TPU v7x, 32 devices: a whole 2x2x4 slice. The times are simulated.
32 devices in a mesh: ctx: 16 (over z, y, x), kv: 2 (over core).
Axes of the slice: x: 2, y: 2, z: 4, core: 2. Of those that a mesh axis runs over, the one named last changes fastest.
Arguments:
- cache_keys: bfloat16 [8192, 1024], P('ctx', 'kv'), may hold values from -6 to 6
- cache_values: bfloat16 [8192, 1024], P('ctx', 'kv'), may hold values from -6 to 6
- importance: bfloat16 [8, 8192], P('kv', 'ctx'), may hold values from 0.099609375 to 10
- assignment: int32 [8192], P('ctx'), may hold values from 0 to 8191, as said below
- queries: bfloat16 [128, 8192], P(None, 'kv'), may hold values from -40 to 40
Outputs:
- merged_keys: bfloat16 [8192, 1024], P('ctx', 'kv')
- merged_values: bfloat16 [8192, 1024], P('ctx', 'kv')
- attended: bfloat16 [128, 8192], P(None, 'kv')
Inputs may be any that keep to these rules, and one draw needn't show every extreme that they name: `assignment`: each entry is the row itself (the row is kept) or a kept row other than itself (the row is evicted and merges into it). The first row of every aligned block of 128 rows is kept and no row merges into it; in every aligned block between a quarter and five twelfths of the rows, rounded down, are evicted. A shard is an aligned block of 512 rows; shard numbers are taken modulo the number of shards. Of the rows of one shard, at most 16 merge into rows of the shard before it and at most 16 into rows of the shard after it, and into rows of every other shard at least 0 and at most 1. The bounds 16 and 1 are reached in every draw.
All inputs are finite; a program needn't handle non-finite values.
Results may differ from a plain program's by a relative error of at most 0.0055.
Values may be sent and summed in bfloat16 or wider, within the bound.
A program may use at most 192 MiB of HBM per device.

v0:
```python
import jax
import jax.numpy as jnp
from jax import lax
from jax.sharding import PartitionSpec as P

BLOCK = 128
NEAR = 16


def bucket_ranks(bucket, bucket_count):
    row_count = bucket.shape[0]
    block_count = row_count // BLOCK
    labels = jnp.arange(bucket_count, dtype=jnp.int32)
    onehot = (bucket.reshape(block_count, 1, BLOCK) == labels[None, :, None]).astype(jnp.bfloat16)
    earlier = (jnp.arange(BLOCK)[:, None] < jnp.arange(BLOCK)[None, :]).astype(jnp.bfloat16)
    within = jnp.einsum("bnr,rs->bns", onehot, earlier, preferred_element_type=jnp.float32)
    widened = onehot.astype(jnp.float32)
    totals = jnp.sum(widened, axis=2)
    offsets = jnp.cumsum(totals, axis=0) - totals
    ranked = jnp.sum(widened * (within + offsets[:, :, None]), axis=1)
    return ranked.reshape(row_count).astype(jnp.int32)


def pack_rows(payload, slot_index, capacity):
    return tuple(
        (
            jnp.zeros((capacity,) + member.shape[1:], member.dtype)
            .at[slot_index]
            .set(member, mode="drop")
            for member in payload
        )
    )


def fold_peers(members, peers):
    return tuple(
        (member.reshape((peers, member.shape[0] // peers) + member.shape[1:]) for member in members)
    )


def unfold_peers(members):
    return tuple(
        (
            member.reshape((member.shape[0] * member.shape[1],) + member.shape[2:])
            for member in members
        )
    )


def split_target(target_rows):
    high_part = (target_rows // 128).astype(jnp.bfloat16)
    low_part = (target_rows % 128).astype(jnp.bfloat16)
    return (high_part, low_part)


def add_rows(partial_sums, arrived):
    numer_keys, numer_values, denominator = partial_sums
    key_rows, value_rows, weight_rows, high_part, low_part = arrived
    target_rows = high_part.astype(jnp.int32) * 128 + low_part.astype(jnp.int32)
    scale_rows = weight_rows.astype(jnp.float32)
    numer_keys = numer_keys.at[target_rows].add(
        key_rows.astype(jnp.float32) * scale_rows[:, None], mode="drop"
    )
    numer_values = numer_values.at[target_rows].add(
        value_rows.astype(jnp.float32) * scale_rows[:, None], mode="drop"
    )
    denominator = denominator.at[target_rows].add(scale_rows, mode="drop")
    return (numer_keys, numer_values, denominator)


def per_device(cache_keys, cache_values, importance, assignment, queries):
    row_count = cache_keys.shape[0]
    row_width = cache_keys.shape[1]
    kv_local = importance.shape[0]
    head_dim = row_width // kv_local
    shards = lax.axis_size("ctx")
    shard_index = lax.axis_index("ctx")
    row_weight = lax.psum(jnp.sum(importance.astype(jnp.float32), axis=0), "kv").astype(
        jnp.bfloat16
    )
    own_rows = shard_index * row_count + jnp.arange(row_count, dtype=jnp.int32)
    kept_rows = assignment == own_rows
    owner_shard = assignment // row_count
    target = assignment % row_count
    distance = (owner_shard - shard_index) % shards
    at_home = distance == 0
    partial_sums = (
        jnp.zeros((row_count, row_width), jnp.float32),
        jnp.zeros((row_count, row_width), jnp.float32),
        jnp.zeros((row_count,), jnp.float32),
    )
    home_high, home_low = split_target(jnp.where(at_home, target, row_count))
    partial_sums = add_rows(
        partial_sums, (cache_keys, cache_values, row_weight, home_high, home_low)
    )
    bucket_rank = bucket_ranks(distance, shards)
    target_high, target_low = split_target(target)
    payload = (cache_keys, cache_values, row_weight, target_high, target_low)
    slot_index = jnp.where(at_home, shards * NEAR, owner_shard * NEAR + bucket_rank)
    outgoing = fold_peers(pack_rows(payload, slot_index, shards * NEAR), shards)
    incoming = (
        lax.all_to_all(outgoing[0], "ctx", split_axis=0, concat_axis=0, tiled=True),
        lax.all_to_all(outgoing[1], "ctx", split_axis=0, concat_axis=0, tiled=True),
        lax.all_to_all(outgoing[2], "ctx", split_axis=0, concat_axis=0, tiled=True),
        lax.all_to_all(outgoing[3], "ctx", split_axis=0, concat_axis=0, tiled=True),
        lax.all_to_all(outgoing[4], "ctx", split_axis=0, concat_axis=0, tiled=True),
    )
    partial_sums = add_rows(partial_sums, unfold_peers(incoming))
    numer_keys, numer_values, denominator = partial_sums
    safe_total = jnp.where(kept_rows, denominator, 1.0)[:, None]
    merged_keys = jnp.where(
        kept_rows[:, None], numer_keys / safe_total, cache_keys.astype(jnp.float32)
    ).astype(jnp.bfloat16)
    merged_values = jnp.where(
        kept_rows[:, None], numer_values / safe_total, cache_values.astype(jnp.float32)
    ).astype(jnp.bfloat16)
    query_rows = queries.shape[0]
    group_size = queries.shape[1] // row_width
    query_heads = (
        queries.reshape(query_rows, kv_local, group_size, head_dim)
        .transpose(1, 0, 2, 3)
        .reshape(kv_local, query_rows * group_size, head_dim)
    )
    block_span = min(512, row_count)
    span_count = row_count // block_span
    score_scale = head_dim ** (-0.5)

    def advance(block_index, running):
        peak_score, weight_sum, accumulated = running
        key_piece = merged_keys.reshape(block_span, kv_local, head_dim)
        value_piece = merged_values.reshape(block_span, kv_local, head_dim)
        scores = (
            jnp.einsum("hqd,khd->hqk", query_heads, key_piece, preferred_element_type=jnp.float32)
            * score_scale
        )
        scores = jnp.where(kept_rows[None, None, :], scores, -jnp.inf)
        new_peak = jnp.maximum(peak_score, jnp.max(scores, axis=2))
        weights = jnp.exp(scores - new_peak[:, :, None])
        rescale = jnp.exp(peak_score - new_peak)
        weight_sum = weight_sum * rescale + jnp.sum(weights, axis=2)
        accumulated = accumulated * rescale[:, :, None] + jnp.einsum(
            "hqk,khd->hqd",
            weights.astype(jnp.bfloat16),
            value_piece,
            preferred_element_type=jnp.float32,
        )
        return (new_peak, weight_sum, accumulated)

    pair_rows = query_rows * group_size
    start_state = (
        jnp.full((kv_local, pair_rows), -jnp.inf, jnp.float32),
        jnp.zeros((kv_local, pair_rows), jnp.float32),
        jnp.zeros((kv_local, pair_rows, head_dim), jnp.float32),
    )
    peak_score, weight_sum, accumulated = lax.fori_loop(0, span_count, advance, start_state)
    global_peak = lax.pmax(peak_score, "ctx")
    rescale = jnp.exp(peak_score - global_peak)
    weight_sum, accumulated = lax.psum(
        (weight_sum * rescale, accumulated * rescale[:, :, None]), "ctx"
    )
    finished = accumulated / weight_sum[:, :, None]
    attended = (
        finished.reshape(kv_local, query_rows, group_size, head_dim)
        .transpose(1, 0, 2, 3)
        .reshape(query_rows, kv_local * group_size * head_dim)
        .astype(jnp.bfloat16)
    )
    return (merged_keys, merged_values, attended)


def solution(mesh):
    placed = (P("ctx", "kv"), P("ctx", "kv"), P("kv", "ctx"), P("ctx"), P(None, "kv"))
    return jax.shard_map(
        per_device,
        mesh=mesh,
        in_specs=placed,
        out_specs=(P("ctx", "kv"), P("ctx", "kv"), P(None, "kv")),
        check_vma=False,
    )
```

profile of v0, /device:TPU:0, one launch (start us, length us, event | category | flops | bytes accessed | tf_op | source)
XLA Modules:
  0.0 319.8 jit_solution(6837680007074012929)
XLA Ops:
  12.2 3.8 %scatter_custom_fusion.4 = bf16[256]{0:T(256)(128)(2,1)S(1)} fusion(s32[512]{0:T(512)S(1)} %get-tuple-element.38, bf16[512]{0:T(512)(128)(2,1)S(1)} %psum.21, bf16[]{:T(256)} %constant.109.clone.1), kind=kCustom, calls=%fused_computation.111 | custom fusion | bytes 514 | tf_op jit(solution)/shard_map/scatter | solution.py:29
  16.7 8.2 %all-to-all-start.3 = ((bf16[16,1,16]{2,1,0:T(2,128)(2,1)}), bf16[16,1,16]{2,1,0:T(2,128)(2,1)S(1)}, u32[]{:S(2)}, u32[]{:S(2)}) async-start(bf16[16,1,16]{2,1,0:T(2,128)(2,1)} %all_to_all.34), calls=%async_computation.3 | async-start | bytes 16384 | tf_op jit(solution)/shard_map/all_to_all | solution.py:104
  24.9 3.8 %scatter_custom_fusion.1 = bf16[256]{0:T(256)(128)(2,1)S(1)} fusion(s32[512]{0:T(512)S(1)} %get-tuple-element.38, bf16[512]{0:T(512)(128)(2,1)S(1)} %get-tuple-element.36, bf16[]{:T(256)} %constant.109.clone.1), kind=kCustom, calls=%fused_computation.115 | custom fusion | bytes 514 | tf_op jit(solution)/shard_map/scatter | solution.py:29
  29.4 2.7 all-to-all-done.3
  32.1 4.2 %all-to-all-start = ((bf16[16,1,16]{2,1,0:T(2,128)(2,1)}), bf16[16,1,16]{2,1,0:T(2,128)(2,1)S(1)}, u32[]{:S(2)}, u32[]{:S(2)}) async-start(bf16[16,1,16]{2,1,0:T(2,128)(2,1)} %all_to_all.32), calls=%async_computation | async-start | bytes 16384 | tf_op jit(solution)/shard_map/all_to_all | solution.py:105
  36.3 3.8 %scatter_custom_fusion.2 = bf16[256]{0:T(256)(128)(2,1)S(1)} fusion(s32[512]{0:T(512)S(1)} %get-tuple-element.38, bf16[512]{0:T(512)(128)(2,1)S(1)} %get-tuple-element.37, bf16[]{:T(256)} %constant.109.clone.1), kind=kCustom, calls=%fused_computation.113 | custom fusion | bytes 514 | tf_op jit(solution)/shard_map/scatter | solution.py:29
  43.5 4.2 %all-to-all-start.1 = ((bf16[16,1,16]{2,1,0:T(2,128)(2,1)}), bf16[16,1,16]{2,1,0:T(2,128)(2,1)S(1)}, u32[]{:S(2)}, u32[]{:S(2)}) async-start(bf16[16,1,16]{2,1,0:T(2,128)(2,1)} %all_to_all.33), calls=%async_computation.1 | async-start | bytes 16384 | tf_op jit(solution)/shard_map/all_to_all | solution.py:106
  47.7 3.5 %scatter_custom_fusion.3 = bf16[256,512]{1,0:T(8,128)(2,1)} fusion(s32[512]{0:T(512)S(1)} %get-tuple-element.38, bf16[512,512]{1,0:T(8,128)(2,1)} %param.5, bf16[]{:T(256)} %constant.109.clone.1), kind=kCustom, calls=%fused_computation.56 | custom fusion | bytes 262656 | tf_op jit(solution)/shard_map/scatter | solution.py:29
  51.2 3.7 %all-to-all-done.1 = bf16[16,1,16]{2,1,0:T(2,128)(2,1)S(1)} async-done(((bf16[16,1,16]{2,1,0:T(2,128)(2,1)}), bf16[16,1,16]{2,1,0:T(2,128)(2,1)S(1)}, u32[]{:S(2)}, u32[]{:S(2)}) %all-to-all-start.1) | async-done | bytes 544 | tf_op jit(solution)/shard_map/all_to_all | solution.py:106
  54.9 3.5 %all-to-all-start.2 = ((bf16[16,16,512]{2,1,0:T(8,128)(2,1)}), bf16[16,16,512]{2,1,0:T(8,128)(2,1)S(1)}, u32[]{:S(2)}, u32[]{:S(2)}) async-start(bf16[16,16,512]{2,1,0:T(8,128)(2,1)} %bitcast.4), calls=%async_computation.2 | async-start | bytes 524288 | tf_op jit(solution)/shard_map/all_to_all | solution.py:102
  59.1 4.1 %scatter_custom_fusion.6 = f32[512]{0:T(512)S(1)} fusion(s32[512]{0:T(512)S(1)} %compare_select_fusion.2, f32[512]{0:T(512)S(1)} %convert_element_type.121, f32[]{:T(128)} %constant.98.clone.1), kind=kCustom, calls=%fused_computation.106 | custom fusion | flops 512 | bytes 2052 | tf_op jit(solution)/shard_map/scatter-add | solution.py:67
  63.2 4.5 %scatter_custom_fusion = f32[512,512]{1,0:T(8,128)S(1)} fusion(s32[512]{0:T(512)S(1)} %compare_select_fusion.2, bf16[512,512]{1,0:T(8,128)(2,1)} %param.5, f32[512]{0:T(512)S(1)} %convert_element_type.121, f32[]{:T(128)} %constant.98.clone.1), kind=kCustom, calls=%fused_computation.31 | custom fusion | flops 786432 | bytes 1574916 | tf_op jit(solution)/shard_map/scatter-add | solution.py:61
  67.7 3.5 %scatter_custom_fusion.9 = bf16[256,512]{1,0:T(8,128)(2,1)} fusion(s32[512]{0:T(512)S(1)} %get-tuple-element.38, bf16[512,512]{1,0:T(8,128)(2,1)} %param.6, bf16[]{:T(256)} %constant.109.clone.1), kind=kCustom, calls=%fused_computation.54 | custom fusion | bytes 262656 | tf_op jit(solution)/shard_map/scatter | solution.py:29
  71.2 4.5 %scatter_custom_fusion.8 = f32[512,512]{1,0:T(8,128)S(1)} fusion(s32[512]{0:T(512)S(1)} %compare_select_fusion.2, bf16[512,512]{1,0:T(8,128)(2,1)} %param.6, f32[512]{0:T(512)S(1)} %convert_element_type.121, f32[]{:T(128)} %constant.98.clone.1), kind=kCustom, calls=%fused_computation.33 | custom fusion | flops 786432 | bytes 1574916 | tf_op jit(solution)/shard_map/scatter-add | solution.py:64
  77.2 6.9 %all-to-all-start.4 = ((bf16[16,16,512]{2,1,0:T(8,128)(2,1)}), bf16[16,16,512]{2,1,0:T(8,128)(2,1)}, u32[]{:S(2)}, u32[]{:S(2)}) async-start(bf16[16,16,512]{2,1,0:T(8,128)(2,1)} %bitcast.6), calls=%async_computation.4 | async-start | bytes 524288 | tf_op jit(solution)/shard_map/all_to_all | solution.py:103
  86.7 2.8 scatter_custom_fusion.5
  89.5 3.2 %all-to-all-done.4 = bf16[16,16,512]{2,1,0:T(8,128)(2,1)} async-done(((bf16[16,16,512]{2,1,0:T(8,128)(2,1)}), bf16[16,16,512]{2,1,0:T(8,128)(2,1)}, u32[]{:S(2)}, u32[]{:S(2)}) %all-to-all-start.4) | async-done | bytes 262176 | tf_op jit(solution)/shard_map/all_to_all | solution.py:103
  92.7 3.1 scatter_custom_fusion.10
  98.2 4.5 %bitcast_reduce_fusion = (f32[4,1024]{1,0:T(4,128)S(1)}, f32[4,512,1024]{2,1,0:T(8,128)}) fusion(pred[512]{0:T(512)(128)(4,1)S(1)} %get-tuple-element.22, bf16[4,128,8,128]{3,2,0,1:T(8,128)(2,1)S(1)} %bitcast.70, bf16[512,512]{1,0:T(8,128)(2,1)S(1)} %get-tuple-element.35), kind=kOutput, calls=%fused_computation.12 | convolution fusion | flops 543158272 | bytes 9978368 | tf_op jit(solution)/shard_map/while/body/eval_jaxpr/hqd,khd->hqk/dot_general | solution.py:133
  102.7 73.9 %pmax.7 = f32[4,1024]{1,0:T(4,128)S(1)} all-reduce(f32[4,1024]{1,0:T(4,128)S(1)} %get-tuple-element.40), channel_id=1, replica_groups=mesh['ctx'=16,'kv'=2] {'ctx'}, use_global_device_ids=true, to_apply=%region_17.18 | all-reduce | flops 4096 | bytes 32768 | tf_op jit(solution)/shard_map/pmax | solution.py:156
  176.6 4.6 %fusion.1 = f32[4,1024]{1,0:T(4,128)S(1)} fusion(f32[4,512,1024]{2,1,0:T(8,128)} %get-tuple-element.41, f32[4,1024]{1,0:T(4,128)S(1)} %get-tuple-element.40, pred[512]{0:T(512)(128)(4,1)S(1)} %get-tuple-element.22), kind=kLoop, calls=%fused_computation.15 | loop fusion | flops 8384512 | bytes 8421888 | tf_op jit(solution)/shard_map/while/body/eval_jaxpr/reduce_sum | solution.py:140
  182.4 4.5 %add_multiply_fusion = f32[4,1024,128]{2,1,0:T(8,128)} fusion(f32[4,512,1024]{2,1,0:T(8,128)S(1)} %copy-done, f32[4,1024]{1,0:T(4,128)S(1)} %get-tuple-element.40, pred[512]{0:T(512)(128)(4,1)S(1)} %get-tuple-element.22, f32[4,1024]{1,0:T(4,128)S(1)} %get-tuple-element.20, f32[4,1024]{1,0:T(4,128)S(1)} %get-tuple-element.33, bf16[512,512]{1,0:T(8,128)(2,1)S(1)} %copy-done.2), kind=kOutput, calls=%fused_computation.23 | convolution fusion | flops 546308096 | bytes 11059712 | tf_op jit(solution)/shard_map/while/body/eval_jaxpr/hqk,khd->hqd/dot_general | solution.py:141
  186.9 72.8 %psum.23 = f32[4,1024]{1,0:T(4,128)S(1)} all-reduce(f32[4,1024]{1,0:T(4,128)S(1)} %get-tuple-element.19), channel_id=1, replica_groups=mesh['ctx'=16,'kv'=2] {'ctx'}, use_global_device_ids=true, to_apply=%region_20.21 | all-reduce | flops 4096 | bytes 32768 | tf_op jit(solution)/shard_map/psum | solution.py:158
  259.6 49.7 %all-reduce.2.cloned.1.call-done = f32[4,1024,128]{2,1,0:T(8,128)} async-done(((f32[4,1024,128]{2,1,0:T(8,128)}), f32[4,1024,128]{2,1,0:T(8,128)}) %all-reduce.2.cloned.1.call-update) | async-done | bytes 2097168 | tf_op jit(solution)/shard_map/psum | solution.py:158
  (38 shorter events, 21.8 us)
Async XLA Ops:
  7.2 79.5 %copy-start.3 = (s32[512]{0:T(512)S(1)}, s32[512]{0:T(512)}, u32[]{:S(2)}) copy-start(s32[512]{0:T(512)} %param.8) | copy-start | bytes 6148
  16.7 15.4 %all-to-all-start.3 = ((bf16[16,1,16]{2,1,0:T(2,128)(2,1)}), bf16[16,1,16]{2,1,0:T(2,128)(2,1)S(1)}, u32[]{:S(2)}, u32[]{:S(2)}) async-start(bf16[16,1,16]{2,1,0:T(2,128)(2,1)} %all_to_all.34), calls=%async_computation.3 | async-start | bytes 16384 | tf_op jit(solution)/shard_map/all_to_all | solution.py:104
  32.1 11.4 %all-to-all-start = ((bf16[16,1,16]{2,1,0:T(2,128)(2,1)}), bf16[16,1,16]{2,1,0:T(2,128)(2,1)S(1)}, u32[]{:S(2)}, u32[]{:S(2)}) async-start(bf16[16,1,16]{2,1,0:T(2,128)(2,1)} %all_to_all.32), calls=%async_computation | async-start | bytes 16384 | tf_op jit(solution)/shard_map/all_to_all | solution.py:105
  43.5 11.4 %all-to-all-start.1 = ((bf16[16,1,16]{2,1,0:T(2,128)(2,1)}), bf16[16,1,16]{2,1,0:T(2,128)(2,1)S(1)}, u32[]{:S(2)}, u32[]{:S(2)}) async-start(bf16[16,1,16]{2,1,0:T(2,128)(2,1)} %all_to_all.33), calls=%async_computation.1 | async-start | bytes 16384 | tf_op jit(solution)/shard_map/all_to_all | solution.py:106
  54.9 22.3 %all-to-all-start.2 = ((bf16[16,16,512]{2,1,0:T(8,128)(2,1)}), bf16[16,16,512]{2,1,0:T(8,128)(2,1)S(1)}, u32[]{:S(2)}, u32[]{:S(2)}) async-start(bf16[16,16,512]{2,1,0:T(8,128)(2,1)} %bitcast.4), calls=%async_computation.2 | async-start | bytes 524288 | tf_op jit(solution)/shard_map/all_to_all | solution.py:102
  77.2 15.5 %all-to-all-start.4 = ((bf16[16,16,512]{2,1,0:T(8,128)(2,1)}), bf16[16,16,512]{2,1,0:T(8,128)(2,1)}, u32[]{:S(2)}, u32[]{:S(2)}) async-start(bf16[16,16,512]{2,1,0:T(8,128)(2,1)} %bitcast.6), calls=%async_computation.4 | async-start | bytes 524288 | tf_op jit(solution)/shard_map/all_to_all | solution.py:103
  84.1 225.2 %all-reduce.2.cloned.1.call-start = ((), (), s32[]{:S(2)}) async-start(), calls=%async_computation.5 | async-start | bytes 4194304 | tf_op jit(solution)/shard_map/psum | solution.py:158
  98.2 4.5 %copy-start.1 = (bf16[512,512]{1,0:T(8,128)(2,1)}, bf16[512,512]{1,0:T(8,128)(2,1)S(1)}, u32[]{:S(2)}) copy-start(bf16[512,512]{1,0:T(8,128)(2,1)S(1)} %get-tuple-element.35) | copy-start | bytes 1572868
  98.2 83.0 %copy-start.2 = (bf16[512,512]{1,0:T(8,128)(2,1)S(1)}, bf16[512,512]{1,0:T(8,128)(2,1)}, u32[]{:S(2)}) copy-start(bf16[512,512]{1,0:T(8,128)(2,1)} %get-tuple-element.34) | copy-start | bytes 1572868
  176.6 5.8 %copy-start = (f32[4,512,1024]{2,1,0:T(8,128)S(1)}, f32[4,512,1024]{2,1,0:T(8,128)}, u32[]{:S(2)}) copy-start(f32[4,512,1024]{2,1,0:T(8,128)} %get-tuple-element.41) | copy-start | bytes 25165828
Sparse Core Ops, SparseCore 0:
  187.0 122.3 all-reduce.1
where the time goes:
time: 321 us; the launch traced here: 320 us
  blocking collectives  149 us (46%)
  waiting for transfers between devices  62.1 us (19%)
  other arithmetic  33.2 us (10%)
  starting transfers between devices  27.1 us (8%)
  local copies, waits for them, and re-layouts  24.8 us (8%)
  between operations  14.2 us (4%)
  matrix products  9.09 us (3%)
    pmax x1, blocking collectives, per_device(): global_peak = lax.pmax(peak_score, 'ctx')  73.9 us
    psum x1, blocking collectives, per_device(): lax.psum((weight_sum * rescale, accumulated * rescale[:, :, None]), 'ctx')  72.8 us
    psum x1, waiting for transfers between devices, per_device(): lax.psum((weight_sum * rescale, accumulated * rescale[:, :, None]), 'ctx')  49.7 us
    scatter x5, local copies, waits for them, and re-layouts, pack_rows(): return tuple((jnp.zeros((capacity,) + member.shape[1:], member.dtype).at[...  18.3 us
    all_to_all x1, starting transfers between devices, per_device(): lax.all_to_all(outgoing[2], 'ctx', split_axis=0, concat_axis=0, tiled=True)  8.2 us
    scatter-add x2, other arithmetic, add_rows(): numer_values.at[target_rows]  7.6 us
    scatter-add x2, other arithmetic, add_rows(): numer_keys.at[target_rows]  7.2 us
    all_to_all x1, starting transfers between devices, per_device(): lax.all_to_all(outgoing[1], 'ctx', split_axis=0, concat_axis=0, tiled=True)  6.94 us
  transfers between devices with their start and end apart: 6, of which 5 were waited for; matrix products, arithmetic and copies ran while one was open for 11% of the time, Pallas kernels for 0%

commit v1 on v0

v1 whole, which is shorter than its diff:
```python
import functools
import math

import jax
import jax.numpy as jnp
from jax import lax
from jax.experimental import pallas as pl
from jax.experimental.pallas import tpu as pltpu
from jax.sharding import PartitionSpec as P

NEAR = 16
LANES = 128
PLANE = 4
MESH = pl.DeviceIdType.MESH
F32 = jnp.float32
BF16 = jnp.bfloat16


def dot(a, b):
    return jnp.dot(a, b, preferred_element_type=F32)


def dot_t(a, b):
    return lax.dot_general(a, b, (((0,), (0,)), ((), ())), preferred_element_type=F32)


def flip(index, step):
    if step == 1:
        return index + 1 - 2 * lax.rem(index, 2)
    if step == 2:
        return index + 2 - 4 * lax.div(index, 2)
    return 3 - index


def combine(parts, coef):
    peak = functools.reduce(jnp.maximum, [m for _, m, _ in parts])
    total, weight = None, None
    for o, m, l in parts:
        factor = jnp.exp2((m - peak) * coef)
        o, l = o * factor, l * factor
        total = o if total is None else total + o
        weight = l if weight is None else weight + l
    return total, peak, weight


def stats(m, l):
    rows = lax.broadcasted_iota(jnp.int32, (8, m.shape[1]), 0)
    shape = (8, m.shape[1])
    return jnp.where(rows == 0, jnp.broadcast_to(m, shape), jnp.broadcast_to(l, shape))


def kernel(
    shards, kv_size, subs, piece,
    k_ref, v_ref, imp_ref, asg_ref, q_ref,
    mk_ref, mv_ref, out_ref,
    kv_send, kv_recv, near_send, near_recv, far_send, far_recv, far_wide, arrived,
    num, q_t, k_ext, v_t,
    l1_send, l1_recv, s1_send, s1_recv, own_o, own_s,
    l2_send, l2_recv, s2_send, s2_recv,
    kv_ss, kv_rs, near_ss, near_rs, far_ss, far_rs,
    l1_ss, l1_rs, s1_ss, s1_rs, l2_ss, l2_rs, s2_ss, s2_rs,
    g2_ss, g2_rs, g1_ss, g1_rs,
):
    me = lax.axis_index("ctx")
    kv = lax.axis_index("kv")
    lo, hi = lax.rem(me, PLANE), lax.div(me, PLANE)
    high = shards // PLANE
    scatter = subs == high
    rows, width = k_ref.shape
    heads = width // LANES
    lanes = q_ref.shape[1]
    group_lanes = lanes // heads
    chunk = lanes // PLANE
    slots = 2 * NEAR + shards
    tiles = 2 * heads
    coef = math.log2(math.e) / math.sqrt(LANES)
    sent = []

    def put(src, dst, ss, rs, target):
        copy = pltpu.make_async_remote_copy(
            src_ref=src, dst_ref=dst, send_sem=ss, recv_sem=rs,
            device_id=target, device_id_type=MESH,
        )
        copy.start()
        sent.append(copy)
        return copy

    barrier = pltpu.get_barrier_semaphore()

    def greet(s, carry):
        pl.semaphore_signal(
            barrier, inc=1, device_id=(lax.rem(me + s, shards), kv), device_id_type=MESH
        )
        return carry

    for s in range(1, kv_size):
        pl.semaphore_signal(
            barrier, inc=1, device_id=(me, lax.rem(kv + s, kv_size)), device_id_type=MESH
        )
    lax.fori_loop(1, shards, greet, 0)

    part_weight = jnp.sum(imp_ref[...].astype(F32), axis=0, keepdims=True)
    kv_send[...] = jnp.broadcast_to(part_weight, (8, rows))
    for s in (0, 1, shards - 1):
        far_recv[s] = jnp.zeros((16, LANES), BF16)
    far_wide[...] = jnp.zeros_like(far_wide)

    pl.semaphore_wait(barrier, shards - 1 + kv_size - 1)
    kv_copies = [
        put(kv_send, kv_recv.at[s], kv_ss.at[s], kv_rs.at[s], (me, lax.rem(kv + s, kv_size)))
        for s in range(1, kv_size)
    ]

    asg = asg_ref[...]
    owner = jnp.right_shift(asg, rows.bit_length() - 1)
    target = jnp.bitwise_and(asg, rows - 1)
    distance = jnp.bitwise_and(owner - me, shards - 1)
    rank_row = lax.broadcasted_iota(jnp.int32, (16, rows), 0)
    distance_16 = jnp.broadcast_to(distance, (16, rows))
    wanted = jnp.where(rank_row == 0, 1, jnp.where(rank_row == 1, shards - 1, -1))
    marks = jnp.where(distance_16 == wanted, 1.0, 0.0).astype(BF16)
    earlier = jnp.where(
        lax.broadcasted_iota(jnp.int32, (rows, rows), 0)
        < lax.broadcasted_iota(jnp.int32, (rows, rows), 1),
        1.0, 0.0,
    ).astype(BF16)
    rank = dot(marks, earlier).astype(jnp.int32)
    key_next = jnp.where(distance == 1, rank[0:1], -1)
    key_prev = jnp.where(distance == shards - 1, rank[1:2], -1)
    far = jnp.where(distance >= 2, jnp.where(distance <= shards - 2, distance, -1), -1)

    def select(key, count):
        index = lax.broadcasted_iota(jnp.int32, (count, rows), 0)
        return jnp.where(jnp.broadcast_to(key, (count, rows)) == index, 1.0, 0.0)

    chosen = jnp.concatenate(
        [select(key_next, NEAR), select(key_prev, NEAR), select(far, shards)], axis=0
    )
    chosen_b = chosen.astype(BF16)
    out_rows = [dot(chosen_b, k_ref[...]), dot(chosen_b, v_ref[...])]
    meta_high = jnp.sum(
        chosen * jnp.right_shift(target, 7).astype(F32), axis=1, keepdims=True
    )
    meta_low = jnp.sum(
        chosen * jnp.bitwise_and(target, LANES - 1).astype(F32), axis=1, keepdims=True
    )
    for d in range(2):
        for part in range(2):
            near_send[d, :, part * width:(part + 1) * width] = out_rows[part][
                d * NEAR:(d + 1) * NEAR
            ].astype(BF16)
    for c in range(tiles):
        part, at = divmod(c, heads)
        far_wide[:, c, :] = out_rows[part][2 * NEAR:, at * LANES:(at + 1) * LANES]

    total_weight = part_weight
    for s, copy in enumerate(kv_copies, 1):
        copy.wait_recv()
        total_weight = total_weight + kv_recv[s, 0:1, :]
    weight = total_weight.astype(BF16).astype(F32)
    meta_weight = jnp.sum(chosen * weight, axis=1, keepdims=True)
    for m, meta in enumerate((meta_weight, meta_high, meta_low)):
        spread = jnp.broadcast_to(meta, (slots, LANES))
        for d in range(2):
            near_send[d, :, 2 * width + m * LANES:2 * width + (m + 1) * LANES] = spread[
                d * NEAR:(d + 1) * NEAR
            ].astype(BF16)
        far_wide[:, tiles + m, :] = spread[2 * NEAR:]
    far_send[...] = far_wide[...].astype(BF16)

    near_copies = [
        put(near_send.at[d], near_recv.at[d], near_ss.at[d], near_rs.at[d],
            (lax.rem(me + step, shards), kv))
        for d, step in enumerate((1, shards - 1))
    ]

    def far_copy(s):
        return pltpu.make_async_remote_copy(
            src_ref=far_send.at[s], dst_ref=far_recv.at[s],
            send_sem=far_ss.at[s], recv_sem=far_rs.at[s],
            device_id=(lax.rem(me + s, shards), kv), device_id_type=MESH,
        )

    def far_start(s, carry):
        far_copy(s).start()
        return carry

    def far_wait(s, carry):
        far_copy(s).wait()
        return carry

    lax.fori_loop(2, shards - 1, far_start, 0)

    home = jnp.where(distance == 0, target, -1)
    home_matrix = jnp.where(
        jnp.broadcast_to(home, (rows, rows))
        == lax.broadcasted_iota(jnp.int32, (rows, rows), 0),
        jnp.broadcast_to(weight, (rows, rows)), 0.0,
    ).astype(BF16)
    num[:, 0:width] = dot(home_matrix, k_ref[...])
    num[:, width:2 * width] = dot(home_matrix, v_ref[...])
    num[:, 2 * width:] = dot(home_matrix, jnp.ones((rows, LANES), BF16))
    for j in range(lanes // LANES):
        at = slice(j * LANES, (j + 1) * LANES)
        q_t[0:LANES, at] = q_ref[:, at].T
    q_t[LANES:, :] = jnp.ones((LANES, lanes), BF16)

    for copy in near_copies:
        copy.wait_recv()
    lax.fori_loop(2, shards - 1, far_wait, 0)

    far_wide[...] = far_recv[...].astype(F32)
    for d in range(2):
        arrived[d * NEAR:(d + 1) * NEAR, 0:2 * width] = near_recv[d, :, 0:2 * width]
    for c in range(tiles):
        arrived[2 * NEAR:, c * LANES:(c + 1) * LANES] = far_wide[:, c, :].astype(BF16)
    arrived[:, 2 * width:] = jnp.ones((slots, LANES), BF16)

    def meta_of(m):
        at = slice(2 * width + m * LANES, 2 * width + (m + 1) * LANES)
        return jnp.concatenate(
            [near_recv[0, :, at].astype(F32), near_recv[1, :, at].astype(F32),
             far_wide[:, tiles + m, :]], axis=0,
        )

    in_weight = meta_of(0)
    in_target = (meta_of(1) * LANES + meta_of(2)).astype(jnp.int32)
    lane = lax.broadcasted_iota(jnp.int32, (slots, LANES), 1)
    spread_t = jnp.concatenate(
        [jnp.where(in_target == lane + b * LANES, in_weight, 0.0) for b in range(rows // LANES)],
        axis=1,
    ).astype(BF16)

    denominator = num[:, 2 * width:] + dot_t(spread_t, arrived[:, 2 * width:])
    kept = denominator > 0.0
    inverse = 1.0 / jnp.where(kept, denominator, 1.0)
    first_lane = lax.broadcasted_iota(jnp.int32, (rows, LANES), 1) == 0
    bias = jnp.where(first_lane, jnp.where(kept, 0.0, -1e30), 0.0).astype(BF16)
    for h in range(heads):
        at = slice(h * LANES, (h + 1) * LANES)
        far_at = slice(width + h * LANES, width + (h + 1) * LANES)
        key = (num[:, at] + dot_t(spread_t, arrived[:, at])) * inverse
        key = jnp.where(kept, key, k_ref[:, at].astype(F32)).astype(BF16)
        mk_ref[:, at] = key
        k_ext[h, :, 0:LANES] = key
        k_ext[h, :, LANES:] = bias
        value = (num[:, far_at] + dot_t(spread_t, arrived[:, far_at])) * inverse
        value = jnp.where(kept, value, v_ref[:, at].astype(F32)).astype(BF16)
        mv_ref[:, at] = value
        v_t[h, 0:LANES, :] = value.T
        v_t[h, LANES:, :] = jnp.ones((16, rows), BF16)

    def attend(column):
        h = lax.div(column, group_lanes)
        queries = q_t[:, pl.ds(pl.multiple_of(column, LANES), piece)]
        score = dot(k_ext[h], queries)
        peak = jnp.max(score, axis=0, keepdims=True)
        prob = jnp.exp2((score - peak) * coef).astype(BF16)
        both = dot(v_t[h], prob)
        return both[0:LANES], peak, both[LANES:LANES + 1]

    def sub_of(u):
        return lax.rem(hi + u, high) if scatter else 0

    order = list(range(1, subs)) + [0]
    l1_copies = {}

    def work(u):
        for s in (3, 1, 2, 0):
            dest = flip(lo, s) if s else lo
            o, m, l = attend(dest * chunk + sub_of(u) * piece)
            if s == 0:
                own_o[u] = o
                own_s[u] = stats(m, l)
                continue
            l1_send[s, u] = o.astype(BF16)
            s1_send[s, u] = stats(m, l)
            to = (hi * PLANE + dest, kv)
            l1_copies[s, u] = (
                put(s1_send.at[s, u], s1_recv.at[s, u], s1_ss.at[s, u], s1_rs.at[s, u], to),
                put(l1_send.at[s, u], l1_recv.at[s, u], l1_ss.at[s, u], l1_rs.at[s, u], to),
            )

    def gather_plane(u):
        parts = [(own_o[u], own_s[u, 0:1, :], own_s[u, 1:2, :])]
        for s in (1, 2, 3):
            for copy in l1_copies[s, u]:
                copy.wait_recv()
            parts.append(
                (l1_recv[s, u].astype(F32), s1_recv[s, u, 0:1, :], s1_recv[s, u, 1:2, :])
            )
        return combine(parts, coef)

    def line(s):
        return (lax.rem(hi + s, high) * PLANE + lo, kv)

    l2_copies = []

    def forward(u):
        o, m, l = gather_plane(u)
        l2_send[u] = o.astype(BF16)
        s2_send[u] = stats(m, l)
        to = line(u)
        l2_copies.append((
            u,
            put(s2_send.at[u], s2_recv.at[u], s2_ss.at[u], s2_rs.at[u], to),
            put(l2_send.at[u], l2_recv.at[u], l2_ss.at[u], l2_rs.at[u], to),
        ))

    for n, u in enumerate(order):
        work(u)
        if n >= 1:
            forward(order[n - 1])

    o, m, l = gather_plane(0)
    if scatter:
        parts = [(o, m, l)]
        for u, first, second in l2_copies:
            first.wait_recv()
            second.wait_recv()
            parts.append((l2_recv[u].astype(F32), s2_recv[u, 0:1, :], s2_recv[u, 1:2, :]))
    else:
        l2_send[0] = o.astype(BF16)
        s2_send[0] = stats(m, l)
        l2_recv[hi] = o.astype(BF16)
        s2_recv[hi] = stats(m, l)
        for s in range(1, high):
            put(s2_send.at[0], s2_recv.at[hi], s2_ss.at[s], s2_rs.at[hi], line(s))
            put(l2_send.at[0], l2_recv.at[hi], l2_ss.at[s], l2_rs.at[hi], line(s))
        for s in range(1, high):
            other = lax.rem(hi + s, high)
            for src, dst, ss, rs in (
                (s2_send, s2_recv, s2_ss, s2_rs), (l2_send, l2_recv, l2_ss, l2_rs),
            ):
                pltpu.make_async_remote_copy(
                    src_ref=src.at[0], dst_ref=dst.at[other], send_sem=ss.at[s],
                    recv_sem=rs.at[other], device_id=line(s), device_id_type=MESH,
                ).wait_recv()
        parts = [
            (l2_recv[j].astype(F32), s2_recv[j, 0:1, :], s2_recv[j, 1:2, :]) for j in range(high)
        ]
    o, m, l = combine(parts, coef)
    result = o * (1.0 / l)
    mine = lo * chunk + sub_of(0) * piece
    for j in range(piece // LANES):
        at = pl.ds(pl.multiple_of(mine + j * LANES, LANES), LANES)
        out_ref[:, at] = result[:, j * LANES:(j + 1) * LANES].T.astype(BF16)

    def block(column):
        return out_ref.at[:, pl.ds(pl.multiple_of(column, LANES), piece)]

    g2_copies = []
    g1_copies = []
    if scatter:
        for s in range(1, high):
            g2_copies.append(
                (s, put(block(mine), block(mine), g2_ss.at[s], g2_rs.at[s], line(s)))
            )

    def to_plane(s, column):
        for p in (3, 1, 2):
            to = (hi * PLANE + flip(lo, p), kv)
            g1_copies.append(
                put(block(column), block(column), g1_ss.at[p, s], g1_rs.at[p, s], to)
            )

    def from_line(s):
        return lo * chunk + lax.rem(hi - s + high, high) * piece if scatter else lo * chunk

    def in_copy(ss, rs, column):
        return pltpu.make_async_remote_copy(
            src_ref=block(column), dst_ref=block(column), send_sem=ss, recv_sem=rs,
            device_id=line(1), device_id_type=MESH,
        )

    to_plane(0, mine)
    for s, _ in g2_copies:
        column = from_line(s)
        in_copy(g2_ss.at[s], g2_rs.at[s], column).wait_recv()
        to_plane(s, column)
    for s in range(subs):
        for p in (1, 2, 3):
            column = from_line(s) + (flip(lo, p) - lo) * chunk
            in_copy(g1_ss.at[p, s], g1_rs.at[p, s], column).wait_recv()
    for copy in sent:
        copy.wait_send()


def per_device(cache_keys, cache_values, importance, assignment, queries):
    shards = lax.axis_size("ctx")
    kv_size = lax.axis_size("kv")
    rows, width = cache_keys.shape
    lanes = queries.shape[1]
    high = shards // PLANE
    subs = high if (lanes // PLANE) % (high * LANES) == 0 else 1
    piece = lanes // PLANE // subs
    heads = width // LANES
    slots = 2 * NEAR + shards
    wide = 2 * width + 3 * LANES
    dma = pltpu.SemaphoreType.DMA
    vmem = pl.BlockSpec(memory_space=pltpu.VMEM)
    body = functools.partial(kernel, shards, kv_size, subs, piece)
    call = pl.pallas_call(
        body,
        out_shape=(
            jax.ShapeDtypeStruct((rows, width), BF16),
            jax.ShapeDtypeStruct((rows, width), BF16),
            jax.ShapeDtypeStruct(queries.shape, BF16),
        ),
        in_specs=[vmem] * 5,
        out_specs=(vmem,) * 3,
        scratch_shapes=[
            pltpu.VMEM((8, rows), F32),
            pltpu.VMEM((kv_size, 8, rows), F32),
            pltpu.VMEM((2, NEAR, wide), BF16),
            pltpu.VMEM((2, NEAR, wide), BF16),
            pltpu.VMEM((shards, 16, LANES), BF16),
            pltpu.VMEM((shards, 16, LANES), BF16),
            pltpu.VMEM((shards, 16, LANES), F32),
            pltpu.VMEM((slots, 2 * width + LANES), BF16),
            pltpu.VMEM((rows, 2 * width + LANES), F32),
            pltpu.VMEM((2 * LANES, lanes), BF16),
            pltpu.VMEM((heads, rows, 2 * LANES), BF16),
            pltpu.VMEM((heads, LANES + 16, rows), BF16),
            pltpu.VMEM((PLANE, subs, LANES, piece), BF16),
            pltpu.VMEM((PLANE, subs, LANES, piece), BF16),
            pltpu.VMEM((PLANE, subs, 8, piece), F32),
            pltpu.VMEM((PLANE, subs, 8, piece), F32),
            pltpu.VMEM((subs, LANES, piece), F32),
            pltpu.VMEM((subs, 8, piece), F32),
            pltpu.VMEM((high, LANES, piece), BF16),
            pltpu.VMEM((high, LANES, piece), BF16),
            pltpu.VMEM((high, 8, piece), F32),
            pltpu.VMEM((high, 8, piece), F32),
            dma((kv_size,)), dma((kv_size,)),
            dma((2,)), dma((2,)),
            dma((shards,)), dma((shards,)),
            dma((PLANE, subs)), dma((PLANE, subs)),
            dma((PLANE, subs)), dma((PLANE, subs)),
            dma((high,)), dma((high,)),
            dma((high,)), dma((high,)),
            dma((high,)), dma((high,)),
            dma((PLANE, subs)), dma((PLANE, subs)),
        ],
        compiler_params=pltpu.CompilerParams(
            collective_id=0, has_side_effects=True, vmem_limit_bytes=40 * 1024 * 1024
        ),
    )
    return call(cache_keys, cache_values, importance, assignment.reshape(1, rows), queries)


def solution(mesh):
    placed = (P("ctx", "kv"), P("ctx", "kv"), P("kv", "ctx"), P("ctx"), P(None, "kv"))
    return jax.shard_map(
        per_device,
        mesh=mesh,
        in_specs=placed,
        out_specs=(P("ctx", "kv"), P("ctx", "kv"), P(None, "kv")),
        check_vma=False,
    )
```

time: 321 us -> 53.8 us (0.17)
  blocking collectives: 149 us -> 0 us
  waiting for transfers between devices: 62.1 us -> 0 us
  Pallas kernels: 0 us -> 45.6 us
  other arithmetic: 33.2 us -> 0 us
  starting transfers between devices: 27.1 us -> 0 us
  local copies, waits for them, and re-layouts: 24.8 us -> 7.23 us
  between operations: 14.2 us -> 0.65 us
  matrix products: 9.09 us -> 0 us
    psum x2 -> x0, blocking collectives: 75.4 us -> none  [the longest x1 72.8 us: per_device(): lax.psum((weight_sum * rescale, accumulated * rescale[:, :, None]), 'ctx')]
    pmax x1 -> x0, blocking collectives: 73.9 us -> none  [per_device(): global_peak = lax.pmax(peak_score, 'ctx')]
    psum x1 -> x0, waiting for transfers between devices: 49.7 us -> none  [per_device(): lax.psum((weight_sum * rescale, accumulated * rescale[:, :, None]), 'ctx')]
    pallas_call x0 -> x1, Pallas kernels: none -> 45.6 us  [per_device(): call(cache_keys, cache_values, importance, assignment.reshape(1, rows), q...]
    all_to_all x5 -> x0, starting transfers between devices: 27 us -> none  [the longest x1 8.2 us: per_device(): lax.all_to_all(outgoing[2], 'ctx', split_axis=0, concat_axis=0, tiled=True)]
    scatter-add x6 -> x0, other arithmetic: 21.2 us -> none  [the longest x2 7.6 us: add_rows(): numer_values.at[target_rows]]
    scatter x5 -> x0, local copies, waits for them, and re-layouts: 18.3 us -> none  [pack_rows(): return tuple((jnp.zeros((capacity,) + member.shape[1:], member.dtype).at[...]
    all_to_all x5 -> x0, waiting for transfers between devices: 12.4 us -> none  [the longest x1 3.68 us: per_device(): lax.all_to_all(outgoing[4], 'ctx', split_axis=0, concat_axis=0, tiled=True)]
  transfers between devices with their start and end apart: 6 -> 0, of which waited for: 5 -> 0; matrix products, arithmetic and copies ran while one was open for 11% -> 0% of each run, Pallas kernels for 0% -> 0%
where the time goes in v1:
time: 53.8 us; the launch traced here: 53.5 us
  Pallas kernels  45.6 us (85%)
  local copies, waits for them, and re-layouts  7.23 us (13%)
  between operations  0.65 us (1%)
    pallas_call x1, Pallas kernels, per_device(): call(cache_keys, cache_values, importance, assignment.reshape(1, rows), q...  45.6 us
    unnamed x13, local copies, waits for them, and re-layouts  7.23 us

profile of v1, /device:TPU:0, one launch (start us, length us, event | category | flops | bytes accessed | tf_op | source)
XLA Modules:
  0.0 53.5 jit_solution(7303128279635605086)
XLA Ops:
  0.6 0.0 copy-start
  0.6 1.2 %copy-done = bf16[128,4096]{1,0:T(8,128)(2,1)S(1)} copy-done((bf16[128,4096]{1,0:T(8,128)(2,1)S(1)}, bf16[128,4096]{1,0:T(8,128)(2,1)}, u32[]{:S(2)}) %copy-start) | copy-done | bytes 1048600
  1.9 0.0 copy-start.1
  1.9 1.0 %copy-done.1 = bf16[512,512]{1,0:T(8,128)(2,1)S(1)} copy-done((bf16[512,512]{1,0:T(8,128)(2,1)S(1)}, bf16[512,512]{1,0:T(8,128)(2,1)}, u32[]{:S(2)}) %copy-start.1) | copy-done | bytes 524312
  2.9 0.0 copy-start.2
  2.9 1.0 %copy-done.2 = bf16[512,512]{1,0:T(8,128)(2,1)S(1)} copy-done((bf16[512,512]{1,0:T(8,128)(2,1)S(1)}, bf16[512,512]{1,0:T(8,128)(2,1)}, u32[]{:S(2)}) %copy-start.2) | copy-done | bytes 524312
  3.9 0.0 copy-start.3
  3.9 0.7 %copy-done.3 = bf16[4,512]{1,0:T(4,128)(2,1)S(1)} copy-done((bf16[4,512]{1,0:T(4,128)(2,1)S(1)}, bf16[4,512]{1,0:T(4,128)(2,1)}, u32[]{:S(2)}) %copy-start.3) | copy-done | bytes 4120
  4.6 0.0 copy-start.4
  4.6 0.7 %copy-done.4 = s32[512]{0:T(512)S(1)} copy-done((s32[512]{0:T(512)S(1)}, s32[512]{0:T(512)}, u32[]{:S(2)}) %copy-start.4) | copy-done | bytes 2072
  5.3 45.6 %shard_map.76 = (bf16[512,512]{1,0:T(8,128)(2,1)S(1)}, bf16[512,512]{1,0:T(8,128)(2,1)S(1)}, bf16[128,4096]{1,0:T(8,128)(2,1)S(1)}) custom-call(bf16[512,512]{1,0:T(8,128)(2,1)S(1)} %copy-done.1, bf16[512,512]{1,0:T(8,128)(2,1)S(1)} %copy-done.2, bf16[4,512]{1,0:T(4,128)(2,1)S(1)} %copy-done.3, s32[1,512]{1,0:T(1,128)S(1)} %bitcast.1, ...), custom_call_target="tpu_custom_call" | custom-call | tf_op jit(solution)/shard_map/pallas_call | solution.py:449
  50.9 0.8 %copy.11 = bf16[512,512]{1,0:T(8,128)(2,1)} copy(bf16[512,512]{1,0:T(8,128)(2,1)S(1)} %get-tuple-element.6) | data formatting | bytes 1048576
  51.7 0.8 %copy.12 = bf16[512,512]{1,0:T(8,128)(2,1)} copy(bf16[512,512]{1,0:T(8,128)(2,1)S(1)} %get-tuple-element.7) | data formatting | bytes 1048576
  52.5 1.0 %copy.13 = bf16[128,4096]{1,0:T(8,128)(2,1)} copy(bf16[128,4096]{1,0:T(8,128)(2,1)S(1)} %get-tuple-element.8) | data formatting | bytes 2097152
Async XLA Ops:
  0.6 1.2 %copy-start = (bf16[128,4096]{1,0:T(8,128)(2,1)S(1)}, bf16[128,4096]{1,0:T(8,128)(2,1)}, u32[]{:S(2)}) copy-start(bf16[128,4096]{1,0:T(8,128)(2,1)} %q_ref.1) | copy-start | bytes 3145732
  1.9 1.0 %copy-start.1 = (bf16[512,512]{1,0:T(8,128)(2,1)S(1)}, bf16[512,512]{1,0:T(8,128)(2,1)}, u32[]{:S(2)}) copy-start(bf16[512,512]{1,0:T(8,128)(2,1)} %k_ref.1) | copy-start | bytes 1572868
  2.9 1.0 %copy-start.2 = (bf16[512,512]{1,0:T(8,128)(2,1)S(1)}, bf16[512,512]{1,0:T(8,128)(2,1)}, u32[]{:S(2)}) copy-start(bf16[512,512]{1,0:T(8,128)(2,1)} %v_ref.1) | copy-start | bytes 1572868
  3.9 0.7 %copy-start.3 = (bf16[4,512]{1,0:T(4,128)(2,1)S(1)}, bf16[4,512]{1,0:T(4,128)(2,1)}, u32[]{:S(2)}) copy-start(bf16[4,512]{1,0:T(4,128)(2,1)} %imp_ref.1) | copy-start | bytes 12292
  4.6 0.7 %copy-start.4 = (s32[512]{0:T(512)S(1)}, s32[512]{0:T(512)}, u32[]{:S(2)}) copy-start(s32[512]{0:T(512)} %param.8) | copy-start | bytes 6148

commit v2 on v1

--- a/solution.py
+++ b/solution.py
@@ -51,8 +51,9 @@
 
 def kernel(
     shards, kv_size, subs, piece,
-    k_ref, v_ref, imp_ref, asg_ref, q_ref,
+    k_hbm, v_hbm, imp_hbm, asg_hbm, q_hbm,
     mk_ref, mv_ref, out_ref,
+    k_ref, v_ref, imp_ref, asg_ref, q_ref, in_sems,
     kv_send, kv_recv, near_send, near_recv, far_send, far_recv, far_wide, arrived,
     num, q_t, k_ext, v_t,
     l1_send, l1_recv, s1_send, s1_recv, own_o, own_s,
@@ -85,6 +86,13 @@
         sent.append(copy)
         return copy
 
+    imp_in, asg_in, k_in, v_in, q_in = [
+        pltpu.make_async_copy(src, dst, in_sems.at[n])
+        for n, (src, dst) in enumerate((
+            (imp_hbm, imp_ref), (asg_hbm, asg_ref), (k_hbm, k_ref), (v_hbm, v_ref),
+            (q_hbm, q_ref),
+        ))
+    ]
     barrier = pltpu.get_barrier_semaphore()
 
     def greet(s, carry):
@@ -98,19 +106,17 @@
             barrier, inc=1, device_id=(me, lax.rem(kv + s, kv_size)), device_id_type=MESH
         )
     lax.fori_loop(1, shards, greet, 0)
-
+    for copy in (imp_in, asg_in, k_in, v_in, q_in):
+        copy.start()
+
+    imp_in.wait()
     part_weight = jnp.sum(imp_ref[...].astype(F32), axis=0, keepdims=True)
     kv_send[...] = jnp.broadcast_to(part_weight, (8, rows))
     for s in (0, 1, shards - 1):
         far_recv[s] = jnp.zeros((16, LANES), BF16)
     far_wide[...] = jnp.zeros_like(far_wide)
 
-    pl.semaphore_wait(barrier, shards - 1 + kv_size - 1)
-    kv_copies = [
-        put(kv_send, kv_recv.at[s], kv_ss.at[s], kv_rs.at[s], (me, lax.rem(kv + s, kv_size)))
-        for s in range(1, kv_size)
-    ]
-
+    asg_in.wait()
     asg = asg_ref[...]
     owner = jnp.right_shift(asg, rows.bit_length() - 1)
     target = jnp.bitwise_and(asg, rows - 1)
@@ -136,7 +142,15 @@
     chosen = jnp.concatenate(
         [select(key_next, NEAR), select(key_prev, NEAR), select(far, shards)], axis=0
     )
+    pl.semaphore_wait(barrier, shards - 1 + kv_size - 1)
+    kv_copies = [
+        put(kv_send, kv_recv.at[s], kv_ss.at[s], kv_rs.at[s], (me, lax.rem(kv + s, kv_size)))
+        for s in range(1, kv_size)
+    ]
+
     chosen_b = chosen.astype(BF16)
+    k_in.wait()
+    v_in.wait()
     out_rows = [dot(chosen_b, k_ref[...]), dot(chosen_b, v_ref[...])]
     meta_high = jnp.sum(
         chosen * jnp.right_shift(target, 7).astype(F32), axis=1, keepdims=True
@@ -200,6 +214,7 @@
     num[:, 0:width] = dot(home_matrix, k_ref[...])
     num[:, width:2 * width] = dot(home_matrix, v_ref[...])
     num[:, 2 * width:] = dot(home_matrix, jnp.ones((rows, LANES), BF16))
+    q_in.wait()
     for j in range(lanes // LANES):
         at = slice(j * LANES, (j + 1) * LANES)
         q_t[0:LANES, at] = q_ref[:, at].T
@@ -349,41 +364,62 @@
     def block(column):
         return out_ref.at[:, pl.ds(pl.multiple_of(column, LANES), piece)]
 
-    g2_copies = []
-    g1_copies = []
     if scatter:
         for s in range(1, high):
-            g2_copies.append(
-                (s, put(block(mine), block(mine), g2_ss.at[s], g2_rs.at[s], line(s)))
-            )
-
-    def to_plane(s, column):
-        for p in (3, 1, 2):
-            to = (hi * PLANE + flip(lo, p), kv)
-            g1_copies.append(
-                put(block(column), block(column), g1_ss.at[p, s], g1_rs.at[p, s], to)
-            )
+            put(block(mine), block(mine), g2_ss.at[s], g2_rs.at[s], line(s))
+
+    half = piece // 2
+
+    def part(column, h):
+        return out_ref.at[:, pl.ds(pl.multiple_of(column + h * half, LANES), half)]
+
+    across = {p: (hi * PLANE + flip(lo, p), kv) for p in (1, 2)}
 
     def from_line(s):
         return lo * chunk + lax.rem(hi - s + high, high) * piece if scatter else lo * chunk
 
-    def in_copy(ss, rs, column):
-        return pltpu.make_async_remote_copy(
-            src_ref=block(column), dst_ref=block(column), send_sem=ss, recv_sem=rs,
+    def beside(s, p):
+        return from_line(s) + (flip(lo, p) - lo) * chunk
+
+    def await_copy(view, ss, rs):
+        pltpu.make_async_remote_copy(
+            src_ref=view, dst_ref=view, send_sem=ss, recv_sem=rs,
             device_id=line(1), device_id_type=MESH,
-        )
-
-    to_plane(0, mine)
-    for s, _ in g2_copies:
-        column = from_line(s)
-        in_copy(g2_ss.at[s], g2_rs.at[s], column).wait_recv()
-        to_plane(s, column)
+        ).wait_recv()
+
+    def to_plane(s):
+        view = block(from_line(s))
+        for p in (1, 2):
+            put(view, view, g1_ss.at[p, s], g1_rs.at[p, s], across[p])
+
+    def pass_on(s):
+        for p, h, over, slot in ((1, 0, 2, 3), (2, 1, 1, 0)):
+            await_copy(block(beside(s, p)), g1_ss.at[p, s], g1_rs.at[p, s])
+            view = part(beside(s, p), h)
+            put(view, view, g1_ss.at[slot, s], g1_rs.at[slot, s], across[over])
+
+    to_plane(0)
+    for s in range(1, subs):
+        await_copy(block(from_line(s)), g2_ss.at[s], g2_rs.at[s])
+        to_plane(s)
+        pass_on(s - 1)
+    pass_on(subs - 1)
     for s in range(subs):
-        for p in (1, 2, 3):
-            column = from_line(s) + (flip(lo, p) - lo) * chunk
-            in_copy(g1_ss.at[p, s], g1_rs.at[p, s], column).wait_recv()
+        for h, slot in ((0, 3), (1, 0)):
+            await_copy(part(beside(s, 3), h), g1_ss.at[slot, s], g1_rs.at[slot, s])
     for copy in sent:
         copy.wait_send()
+
+
+def write_out(mk_ref, mv_ref, out_ref, mk_hbm, mv_hbm, out_hbm, sems):
+    copies = [
+        pltpu.make_async_copy(src, dst, sems.at[n])
+        for n, (src, dst) in enumerate(((out_ref, out_hbm), (mk_ref, mk_hbm), (mv_ref, mv_hbm)))
+    ]
+    for copy in copies:
+        copy.start()
+    for copy in copies:
+        copy.wait()
 
 
 def per_device(cache_keys, cache_values, importance, assignment, queries):
@@ -399,17 +435,25 @@
     wide = 2 * width + 3 * LANES
     dma = pltpu.SemaphoreType.DMA
     vmem = pl.BlockSpec(memory_space=pltpu.VMEM)
+    hbm = pl.BlockSpec(memory_space=pltpu.HBM)
     body = functools.partial(kernel, shards, kv_size, subs, piece)
+    shapes = (
+        jax.ShapeDtypeStruct((rows, width), BF16),
+        jax.ShapeDtypeStruct((rows, width), BF16),
+        jax.ShapeDtypeStruct(queries.shape, BF16),
+    )
     call = pl.pallas_call(
         body,
-        out_shape=(
-            jax.ShapeDtypeStruct((rows, width), BF16),
-            jax.ShapeDtypeStruct((rows, width), BF16),
-            jax.ShapeDtypeStruct(queries.shape, BF16),
-        ),
-        in_specs=[vmem] * 5,
+        out_shape=tuple(pltpu.VMEM(x.shape, x.dtype) for x in shapes),
+        in_specs=[hbm] * 5,
         out_specs=(vmem,) * 3,
         scratch_shapes=[
+            pltpu.VMEM((rows, width), BF16),
+            pltpu.VMEM((rows, width), BF16),
+            pltpu.VMEM(importance.shape, BF16),
+            pltpu.VMEM((1, rows), jnp.int32),
+            pltpu.VMEM(queries.shape, BF16),
+            dma((5,)),
             pltpu.VMEM((8, rows), F32),
             pltpu.VMEM((kv_size, 8, rows), F32),
             pltpu.VMEM((2, NEAR, wide), BF16),
@@ -446,7 +490,15 @@
             collective_id=0, has_side_effects=True, vmem_limit_bytes=40 * 1024 * 1024
         ),
     )
-    return call(cache_keys, cache_values, importance, assignment.reshape(1, rows), queries)
+    operands = (cache_keys, cache_values, importance, assignment.reshape(1, rows), queries)
+    results = call(*(pltpu.with_memory_space_constraint(x, pltpu.HBM) for x in operands))
+    return pl.pallas_call(
+        write_out,
+        out_shape=shapes,
+        in_specs=[vmem] * 3,
+        out_specs=(hbm,) * 3,
+        scratch_shapes=[dma((3,))],
+    )(*results)
 
 
 def solution(mesh):

time: 53.8 us -> 54.1 us (level)
  Pallas kernels: 45.6 us -> 50.7 us
  local copies, waits for them, and re-layouts: 7.23 us -> 2.55 us
    pallas_call x1 -> x2, Pallas kernels: 45.6 us -> 50.7 us  [the longest x1 47.8 us: per_device(): call(*(pltpu.with_memory_space_constraint(x, pltpu.HBM) for x in operands))]
    unnamed x13 -> x6, local copies, waits for them, and re-layouts: 7.23 us -> 2.55 us
where the time goes in v2:
time: 54.1 us; the launch traced here: 53.9 us
  Pallas kernels  50.7 us (94%)
  local copies, waits for them, and re-layouts  2.55 us (5%)
  between operations  0.65 us (1%)
    pallas_call x1, Pallas kernels, per_device(): call(*(pltpu.with_memory_space_constraint(x, pltpu.HBM) for x in operands))  47.8 us
    pallas_call x1, Pallas kernels, per_device(): pl.pallas_call(write_out, out_shape=shapes, in_specs=[vmem] * 3, out_spec...  2.88 us
    unnamed x6, local copies, waits for them, and re-layouts  2.55 us

profile of v2, /device:TPU:0, one launch (start us, length us, event | category | flops | bytes accessed | tf_op | source)
XLA Modules:
  0.0 53.9 jit_solution(8489802743792416664)
XLA Ops:
  0.6 47.8 %shard_map.76 = (bf16[512,512]{1,0:T(8,128)(2,1)S(1)}, bf16[512,512]{1,0:T(8,128)(2,1)S(1)}, bf16[128,4096]{1,0:T(8,128)(2,1)S(1)}) custom-call(bf16[512,512]{1,0:T(8,128)(2,1)} %k_hbm.1, bf16[512,512]{1,0:T(8,128)(2,1)} %v_hbm.1, bf16[4,512]{1,0:T(4,128)(2,1)} %imp_hbm.1, s32[1,512]{1,0:T(1,128)} %bitcast.1, bf16[128,4096]{1,0:T(8,128)(2,1)} %q_hbm.1), custom_call_target="tpu_custom_call" | custom-call | tf_op jit(solution)/shard_map/pallas_call | solution.py:494
  48.4 0.0 copy-start
  48.4 1.0 %copy-done = bf16[128,4096]{1,0:T(8,128)(2,1)} copy-done((bf16[128,4096]{1,0:T(8,128)(2,1)}, bf16[128,4096]{1,0:T(8,128)(2,1)S(1)}, u32[]{:S(2)}) %copy-start) | copy-done | bytes 1048600
  49.4 0.0 copy-start.1
  49.4 0.8 %copy-done.1 = bf16[512,512]{1,0:T(8,128)(2,1)} copy-done((bf16[512,512]{1,0:T(8,128)(2,1)}, bf16[512,512]{1,0:T(8,128)(2,1)S(1)}, u32[]{:S(2)}) %copy-start.1) | copy-done | bytes 524312
  50.2 0.0 copy-start.2
  50.2 0.8 %copy-done.2 = bf16[512,512]{1,0:T(8,128)(2,1)} copy-done((bf16[512,512]{1,0:T(8,128)(2,1)}, bf16[512,512]{1,0:T(8,128)(2,1)S(1)}, u32[]{:S(2)}) %copy-start.2) | copy-done | bytes 524312
  51.0 2.9 %shard_map.77 = (bf16[512,512]{1,0:T(8,128)(2,1)}, bf16[512,512]{1,0:T(8,128)(2,1)}, bf16[128,4096]{1,0:T(8,128)(2,1)}) custom-call(bf16[512,512]{1,0:T(8,128)(2,1)} %copy-done.1, bf16[512,512]{1,0:T(8,128)(2,1)} %copy-done.2, bf16[128,4096]{1,0:T(8,128)(2,1)} %copy-done), custom_call_target="tpu_custom_call" | custom-call | tf_op jit(solution)/shard_map/pallas_call | solution.py:495
Async XLA Ops:
  48.4 1.0 %copy-start = (bf16[128,4096]{1,0:T(8,128)(2,1)}, bf16[128,4096]{1,0:T(8,128)(2,1)S(1)}, u32[]{:S(2)}) copy-start(bf16[128,4096]{1,0:T(8,128)(2,1)S(1)} %get-tuple-element.8.out_ref) | copy-start | bytes 3145732
  49.4 0.8 %copy-start.1 = (bf16[512,512]{1,0:T(8,128)(2,1)}, bf16[512,512]{1,0:T(8,128)(2,1)S(1)}, u32[]{:S(2)}) copy-start(bf16[512,512]{1,0:T(8,128)(2,1)S(1)} %get-tuple-element.6.mk_ref) | copy-start | bytes 1572868
  50.2 0.8 %copy-start.2 = (bf16[512,512]{1,0:T(8,128)(2,1)}, bf16[512,512]{1,0:T(8,128)(2,1)S(1)}, u32[]{:S(2)}) copy-start(bf16[512,512]{1,0:T(8,128)(2,1)S(1)} %get-tuple-element.7.mv_ref) | copy-start | bytes 1572868

commit v3 on v2

--- a/solution.py
+++ b/solution.py
@@ -56,10 +56,10 @@
     k_ref, v_ref, imp_ref, asg_ref, q_ref, in_sems,
     kv_send, kv_recv, near_send, near_recv, far_send, far_recv, far_wide, arrived,
     num, q_t, k_ext, v_t,
-    l1_send, l1_recv, s1_send, s1_recv, own_o, own_s,
+    l1_send, l1_recv, s1_send, s1_recv, h1_send, h1_recv, t1_send, t1_recv, own_o, own_s,
     l2_send, l2_recv, s2_send, s2_recv,
     kv_ss, kv_rs, near_ss, near_rs, far_ss, far_rs,
-    l1_ss, l1_rs, s1_ss, s1_rs, l2_ss, l2_rs, s2_ss, s2_rs,
+    l1_ss, l1_rs, s1_ss, s1_rs, h1_ss, h1_rs, t1_ss, t1_rs, l2_ss, l2_rs, s2_ss, s2_rs,
     g2_ss, g2_rs, g1_ss, g1_rs,
 ):
     me = lax.axis_index("ctx")
@@ -75,6 +75,7 @@
     slots = 2 * NEAR + shards
     tiles = 2 * heads
     coef = math.log2(math.e) / math.sqrt(LANES)
+    half = piece // 2
     sent = []
 
     def put(src, dst, ss, rs, target):
@@ -215,9 +216,14 @@
     num[:, width:2 * width] = dot(home_matrix, v_ref[...])
     num[:, 2 * width:] = dot(home_matrix, jnp.ones((rows, LANES), BF16))
     q_in.wait()
-    for j in range(lanes // LANES):
-        at = slice(j * LANES, (j + 1) * LANES)
-        q_t[0:LANES, at] = q_ref[:, at].T
+
+    def turn_queries(j, carry):
+        at = pl.ds(pl.multiple_of(j * 2 * LANES, 2 * LANES), 2 * LANES)
+        block = q_ref[:, at]
+        q_t[0:LANES, at] = jnp.concatenate([block[:, 0:LANES].T, block[:, LANES:].T], axis=1)
+        return carry
+
+    lax.fori_loop(0, lanes // (2 * LANES), turn_queries, 0)
     q_t[LANES:, :] = jnp.ones((LANES, lanes), BF16)
 
     for copy in near_copies:
@@ -277,62 +283,129 @@
     def sub_of(u):
         return lax.rem(hi + u, high) if scatter else 0
 
-    order = list(range(1, subs)) + [0]
-    l1_copies = {}
+    across = {p: (hi * PLANE + flip(lo, p), kv) for p in (1, 2)}
+    halves = (slice(0, half), slice(half, piece))
+
+    def hop_one(p, u):
+        return [
+            pltpu.make_async_remote_copy(
+                src_ref=src.at[p, u], dst_ref=dst.at[p, u], send_sem=ss.at[p, u],
+                recv_sem=rs.at[p, u], device_id=across[p], device_id_type=MESH,
+            )
+            for src, dst, ss, rs in (
+                (s1_send, s1_recv, s1_ss, s1_rs), (l1_send, l1_recv, l1_ss, l1_rs),
+            )
+        ]
+
+    def hop_two(p, u):
+        return [
+            pltpu.make_async_remote_copy(
+                src_ref=src.at[p, u], dst_ref=dst.at[p, u], send_sem=ss.at[p, u],
+                recv_sem=rs.at[p, u], device_id=across[p], device_id_type=MESH,
+            )
+            for src, dst, ss, rs in (
+                (t1_send, t1_recv, t1_ss, t1_rs), (h1_send, h1_recv, h1_ss, h1_rs),
+            )
+        ]
+
+    def hop_line(u):
+        return [
+            pltpu.make_async_remote_copy(
+                src_ref=src.at[u], dst_ref=dst.at[u], send_sem=ss.at[u],
+                recv_sem=rs.at[u], device_id=line(u), device_id_type=MESH,
+            )
+            for src, dst, ss, rs in (
+                (s2_send, s2_recv, s2_ss, s2_rs), (l2_send, l2_recv, l2_ss, l2_rs),
+            )
+        ]
+
+    def line(s):
+        return (lax.rem(hi + s, high) * PLANE + lo, kv)
+
+    def begin(copies):
+        for copy in copies:
+            copy.start()
 
     def work(u):
         for s in (3, 1, 2, 0):
             dest = flip(lo, s) if s else lo
             o, m, l = attend(dest * chunk + sub_of(u) * piece)
-            if s == 0:
-                own_o[u] = o
-                own_s[u] = stats(m, l)
-                continue
-            l1_send[s, u] = o.astype(BF16)
-            s1_send[s, u] = stats(m, l)
-            to = (hi * PLANE + dest, kv)
-            l1_copies[s, u] = (
-                put(s1_send.at[s, u], s1_recv.at[s, u], s1_ss.at[s, u], s1_rs.at[s, u], to),
-                put(l1_send.at[s, u], l1_recv.at[s, u], l1_ss.at[s, u], l1_rs.at[s, u], to),
-            )
+            st = stats(m, l)
+            if s == 3:
+                for p, h in ((1, 0), (2, 1)):
+                    l1_send[p, u, :, halves[0]] = o[:, halves[h]].astype(BF16)
+                    s1_send[p, u, :, halves[0]] = st[:, halves[h]]
+            elif s == 0:
+                own_o[0, u] = o
+                own_s[0, u] = st
+            else:
+                out, stay = (0, 1) if s == 1 else (1, 0)
+                l1_send[s, u, :, halves[1]] = o[:, halves[out]].astype(BF16)
+                s1_send[s, u, :, halves[1]] = st[:, halves[out]]
+                begin(hop_one(s, u))
+                own_o[s, u, :, halves[0]] = o[:, halves[stay]]
+                own_s[s, u, :, halves[0]] = st[:, halves[stay]]
+
+    def triple(data, extra, u, p, at):
+        return (
+            data[p, u, :, at].astype(F32), extra[p, u, 0:1, at], extra[p, u, 1:2, at]
+        )
+
+    def relay(u):
+        for p in (1, 2):
+            for copy in hop_one(p, u):
+                copy.wait_recv()
+        for p in (1, 2):
+            o, m, l = combine(
+                [triple(own_o, own_s, u, 3 - p, halves[0]),
+                 triple(l1_recv, s1_recv, u, p, halves[0])], coef,
+            )
+            h1_send[3 - p, u] = o.astype(BF16)
+            t1_send[3 - p, u] = stats(m, l)
+            begin(hop_two(3 - p, u))
 
     def gather_plane(u):
-        parts = [(own_o[u], own_s[u, 0:1, :], own_s[u, 1:2, :])]
-        for s in (1, 2, 3):
-            for copy in l1_copies[s, u]:
+        for p in (1, 2):
+            for copy in hop_two(p, u):
                 copy.wait_recv()
-            parts.append(
-                (l1_recv[s, u].astype(F32), s1_recv[s, u, 0:1, :], s1_recv[s, u, 1:2, :])
-            )
-        return combine(parts, coef)
-
-    def line(s):
-        return (lax.rem(hi + s, high) * PLANE + lo, kv)
-
-    l2_copies = []
+        sides = []
+        for p in (1, 2):
+            sides.append(combine(
+                [triple(own_o, own_s, u, 0, halves[p - 1]),
+                 triple(l1_recv, s1_recv, u, p, halves[1]),
+                 triple(h1_recv, t1_recv, u, 3 - p, slice(0, half))], coef,
+            ))
+        return [jnp.concatenate(pair, axis=1) for pair in zip(*sides)]
 
     def forward(u):
         o, m, l = gather_plane(u)
         l2_send[u] = o.astype(BF16)
         s2_send[u] = stats(m, l)
-        to = line(u)
-        l2_copies.append((
-            u,
-            put(s2_send.at[u], s2_recv.at[u], s2_ss.at[u], s2_rs.at[u], to),
-            put(l2_send.at[u], l2_recv.at[u], l2_ss.at[u], l2_rs.at[u], to),
-        ))
-
-    for n, u in enumerate(order):
-        work(u)
-        if n >= 1:
-            forward(order[n - 1])
-
+        begin(hop_line(u))
+
+    def turn(n, carry):
+        work(lax.rem(n + 1, subs))
+
+        @pl.when(n >= 1)
+        def _():
+            relay(n)
+
+        @pl.when(n >= 2)
+        def _():
+            forward(n - 1)
+
+        return carry
+
+    lax.fori_loop(0, subs, turn, 0)
+    relay(0)
+    if scatter:
+        forward(subs - 1)
     o, m, l = gather_plane(0)
     if scatter:
         parts = [(o, m, l)]
-        for u, first, second in l2_copies:
-            first.wait_recv()
-            second.wait_recv()
+        for u in range(1, high):
+            for copy in hop_line(u):
+                copy.wait_recv()
             parts.append((l2_recv[u].astype(F32), s2_recv[u, 0:1, :], s2_recv[u, 1:2, :]))
     else:
         l2_send[0] = o.astype(BF16)
@@ -368,12 +441,8 @@
         for s in range(1, high):
             put(block(mine), block(mine), g2_ss.at[s], g2_rs.at[s], line(s))
 
-    half = piece // 2
-
     def part(column, h):
         return out_ref.at[:, pl.ds(pl.multiple_of(column + h * half, LANES), half)]
-
-    across = {p: (hi * PLANE + flip(lo, p), kv) for p in (1, 2)}
 
     def from_line(s):
         return lo * chunk + lax.rem(hi - s + high, high) * piece if scatter else lo * chunk
@@ -410,16 +479,18 @@
     for copy in sent:
         copy.wait_send()
 
-
-def write_out(mk_ref, mv_ref, out_ref, mk_hbm, mv_hbm, out_hbm, sems):
-    copies = [
-        pltpu.make_async_copy(src, dst, sems.at[n])
-        for n, (src, dst) in enumerate(((out_ref, out_hbm), (mk_ref, mk_hbm), (mv_ref, mv_hbm)))
-    ]
-    for copy in copies:
-        copy.start()
-    for copy in copies:
-        copy.wait()
+    def finish(u, carry):
+        for p in (1, 2):
+            for copy in hop_one(p, u) + hop_two(p, u):
+                copy.wait_send()
+        if scatter:
+            @pl.when(u >= 1)
+            def _():
+                for copy in hop_line(u):
+                    copy.wait_send()
+        return carry
+
+    lax.fori_loop(0, subs, finish, 0)
 
 
 def per_device(cache_keys, cache_values, importance, assignment, queries):
@@ -466,12 +537,16 @@
             pltpu.VMEM((2 * LANES, lanes), BF16),
             pltpu.VMEM((heads, rows, 2 * LANES), BF16),
             pltpu.VMEM((heads, LANES + 16, rows), BF16),
-            pltpu.VMEM((PLANE, subs, LANES, piece), BF16),
-            pltpu.VMEM((PLANE, subs, LANES, piece), BF16),
-            pltpu.VMEM((PLANE, subs, 8, piece), F32),
-            pltpu.VMEM((PLANE, subs, 8, piece), F32),
-            pltpu.VMEM((subs, LANES, piece), F32),
-            pltpu.VMEM((subs, 8, piece), F32),
+            pltpu.VMEM((3, subs, LANES, piece), BF16),
+            pltpu.VMEM((3, subs, LANES, piece), BF16),
+            pltpu.VMEM((3, subs, 8, piece), F32),
+            pltpu.VMEM((3, subs, 8, piece), F32),
+            pltpu.VMEM((3, subs, LANES, piece // 2), BF16),
+            pltpu.VMEM((3, subs, LANES, piece // 2), BF16),
+            pltpu.VMEM((3, subs, 8, piece // 2), F32),
+            pltpu.VMEM((3, subs, 8, piece // 2), F32),
+            pltpu.VMEM((3, subs, LANES, piece), F32),
+            pltpu.VMEM((3, subs, 8, piece), F32),
             pltpu.VMEM((high, LANES, piece), BF16),
             pltpu.VMEM((high, LANES, piece), BF16),
             pltpu.VMEM((high, 8, piece), F32),
@@ -479,8 +554,10 @@
             dma((kv_size,)), dma((kv_size,)),
             dma((2,)), dma((2,)),
             dma((shards,)), dma((shards,)),
-            dma((PLANE, subs)), dma((PLANE, subs)),
-            dma((PLANE, subs)), dma((PLANE, subs)),
+            dma((3, subs)), dma((3, subs)),
+            dma((3, subs)), dma((3, subs)),
+            dma((3, subs)), dma((3, subs)),
+            dma((3, subs)), dma((3, subs)),
             dma((high,)), dma((high,)),
             dma((high,)), dma((high,)),
             dma((high,)), dma((high,)),
@@ -491,14 +568,7 @@
         ),
     )
     operands = (cache_keys, cache_values, importance, assignment.reshape(1, rows), queries)
-    results = call(*(pltpu.with_memory_space_constraint(x, pltpu.HBM) for x in operands))
-    return pl.pallas_call(
-        write_out,
-        out_shape=shapes,
-        in_specs=[vmem] * 3,
-        out_specs=(hbm,) * 3,
-        scratch_shapes=[dma((3,))],
-    )(*results)
+    return call(*(pltpu.with_memory_space_constraint(x, pltpu.HBM) for x in operands))
 
 
 def solution(mesh):

time: 54.1 us -> 51.7 us (0.956)
  Pallas kernels: 50.7 us -> 48.4 us
    pallas_call x1 -> x0, Pallas kernels: 2.88 us -> none  [per_device(): pl.pallas_call(write_out, out_shape=shapes, in_specs=[vmem] * 3, out_spec...]
    pallas_call x1, Pallas kernels: 47.8 us -> 48.4 us  [per_device(): call(*(pltpu.with_memory_space_constraint(x, pltpu.HBM) for x in operands))]
    unnamed x6 -> x3, local copies, waits for them, and re-layouts: 2.55 us -> 2.56 us
where the time goes in v3:
time: 51.7 us; the launch traced here: 51.6 us
  Pallas kernels  48.4 us (94%)
  local copies, waits for them, and re-layouts  2.56 us (5%)
  between operations  0.64 us (1%)
    pallas_call x1, Pallas kernels, per_device(): call(*(pltpu.with_memory_space_constraint(x, pltpu.HBM) for x in operands))  48.4 us
    unnamed x3, local copies, waits for them, and re-layouts  2.56 us

profile of v3, /device:TPU:0, one launch (start us, length us, event | category | flops | bytes accessed | tf_op | source)
XLA Modules:
  0.0 51.6 jit_solution(7675496900505959783)
XLA Ops:
  0.6 48.4 %shard_map.76 = (bf16[512,512]{1,0:T(8,128)(2,1)S(1)}, bf16[512,512]{1,0:T(8,128)(2,1)S(1)}, bf16[128,4096]{1,0:T(8,128)(2,1)S(1)}) custom-call(bf16[512,512]{1,0:T(8,128)(2,1)} %k_hbm.1, bf16[512,512]{1,0:T(8,128)(2,1)} %v_hbm.1, bf16[4,512]{1,0:T(4,128)(2,1)} %imp_hbm.1, s32[1,512]{1,0:T(1,128)} %bitcast.1, bf16[128,4096]{1,0:T(8,128)(2,1)} %q_hbm.1), custom_call_target="tpu_custom_call" | custom-call | tf_op jit(solution)/shard_map/pallas_call | solution.py:571
  49.0 0.8 %copy.11 = bf16[512,512]{1,0:T(8,128)(2,1)} copy(bf16[512,512]{1,0:T(8,128)(2,1)S(1)} %get-tuple-element.3) | data formatting | bytes 1048576
  49.8 0.8 %copy.12 = bf16[512,512]{1,0:T(8,128)(2,1)} copy(bf16[512,512]{1,0:T(8,128)(2,1)S(1)} %get-tuple-element.4) | data formatting | bytes 1048576
  50.6 1.0 %copy.13 = bf16[128,4096]{1,0:T(8,128)(2,1)} copy(bf16[128,4096]{1,0:T(8,128)(2,1)S(1)} %get-tuple-element.5) | data formatting | bytes 2097152

commit v4 on v2

--- a/solution.py
+++ b/solution.py
@@ -50,7 +50,7 @@
 
 
 def kernel(
-    shards, kv_size, subs, piece,
+    shards, kv_size, subs, rounds, piece,
     k_hbm, v_hbm, imp_hbm, asg_hbm, q_hbm,
     mk_ref, mv_ref, out_ref,
     k_ref, v_ref, imp_ref, asg_ref, q_ref, in_sems,
@@ -215,9 +215,16 @@
     num[:, width:2 * width] = dot(home_matrix, v_ref[...])
     num[:, 2 * width:] = dot(home_matrix, jnp.ones((rows, LANES), BF16))
     q_in.wait()
-    for j in range(lanes // LANES):
-        at = slice(j * LANES, (j + 1) * LANES)
-        q_t[0:LANES, at] = q_ref[:, at].T
+
+    def turn_queries(j, carry):
+        at = pl.ds(pl.multiple_of(j * 4 * LANES, 4 * LANES), 4 * LANES)
+        group = q_ref[:, at]
+        q_t[0:LANES, at] = jnp.concatenate(
+            [group[:, n * LANES:(n + 1) * LANES].T for n in range(4)], axis=1
+        )
+        return carry
+
+    lax.fori_loop(0, lanes // (4 * LANES), turn_queries, 0)
     q_t[LANES:, :] = jnp.ones((LANES, lanes), BF16)
 
     for copy in near_copies:
@@ -246,7 +253,8 @@
         axis=1,
     ).astype(BF16)
 
-    denominator = num[:, 2 * width:] + dot_t(spread_t, arrived[:, 2 * width:])
+    num[...] += dot_t(spread_t, arrived[...])
+    denominator = num[:, 2 * width:]
     kept = denominator > 0.0
     inverse = 1.0 / jnp.where(kept, denominator, 1.0)
     first_lane = lax.broadcasted_iota(jnp.int32, (rows, LANES), 1) == 0
@@ -254,12 +262,12 @@
     for h in range(heads):
         at = slice(h * LANES, (h + 1) * LANES)
         far_at = slice(width + h * LANES, width + (h + 1) * LANES)
-        key = (num[:, at] + dot_t(spread_t, arrived[:, at])) * inverse
+        key = num[:, at] * inverse
         key = jnp.where(kept, key, k_ref[:, at].astype(F32)).astype(BF16)
         mk_ref[:, at] = key
         k_ext[h, :, 0:LANES] = key
         k_ext[h, :, LANES:] = bias
-        value = (num[:, far_at] + dot_t(spread_t, arrived[:, far_at])) * inverse
+        value = num[:, far_at] * inverse
         value = jnp.where(kept, value, v_ref[:, at].astype(F32)).astype(BF16)
         mv_ref[:, at] = value
         v_t[h, 0:LANES, :] = value.T
@@ -277,109 +285,99 @@
     def sub_of(u):
         return lax.rem(hi + u, high) if scatter else 0
 
-    order = list(range(1, subs)) + [0]
+    wide = rounds * piece
+
+    def place(part, sub, r):
+        return part * chunk + sub * wide + r * piece
+
+    def line(s):
+        return (lax.rem(hi + s, high) * PLANE + lo, kv)
+
+    across = {p: (hi * PLANE + flip(lo, p), kv) for p in (1, 2, 3)}
     l1_copies = {}
 
-    def work(u):
+    def work(r, u):
+        t = r * subs + u
         for s in (3, 1, 2, 0):
             dest = flip(lo, s) if s else lo
-            o, m, l = attend(dest * chunk + sub_of(u) * piece)
+            o, m, l = attend(place(dest, sub_of(u), r))
             if s == 0:
-                own_o[u] = o
-                own_s[u] = stats(m, l)
+                own_o[t] = o
+                own_s[t] = stats(m, l)
                 continue
-            l1_send[s, u] = o.astype(BF16)
-            s1_send[s, u] = stats(m, l)
-            to = (hi * PLANE + dest, kv)
-            l1_copies[s, u] = (
-                put(s1_send.at[s, u], s1_recv.at[s, u], s1_ss.at[s, u], s1_rs.at[s, u], to),
-                put(l1_send.at[s, u], l1_recv.at[s, u], l1_ss.at[s, u], l1_rs.at[s, u], to),
+            l1_send[s, t] = o.astype(BF16)
+            s1_send[s, t] = stats(m, l)
+            l1_copies[s, t] = (
+                put(s1_send.at[s, t], s1_recv.at[s, t], s1_ss.at[s, t], s1_rs.at[s, t], across[s]),
+                put(l1_send.at[s, t], l1_recv.at[s, t], l1_ss.at[s, t], l1_rs.at[s, t], across[s]),
             )
 
-    def gather_plane(u):
-        parts = [(own_o[u], own_s[u, 0:1, :], own_s[u, 1:2, :])]
+    def gather_plane(r, u):
+        t = r * subs + u
+        parts = [(own_o[t], own_s[t, 0:1, :], own_s[t, 1:2, :])]
         for s in (1, 2, 3):
-            for copy in l1_copies[s, u]:
+            for copy in l1_copies[s, t]:
                 copy.wait_recv()
             parts.append(
-                (l1_recv[s, u].astype(F32), s1_recv[s, u, 0:1, :], s1_recv[s, u, 1:2, :])
+                (l1_recv[s, t].astype(F32), s1_recv[s, t, 0:1, :], s1_recv[s, t, 1:2, :])
             )
         return combine(parts, coef)
 
-    def line(s):
-        return (lax.rem(hi + s, high) * PLANE + lo, kv)
-
     l2_copies = []
 
-    def forward(u):
-        o, m, l = gather_plane(u)
-        l2_send[u] = o.astype(BF16)
-        s2_send[u] = stats(m, l)
-        to = line(u)
+    def forward(r, u):
+        o, m, l = gather_plane(r, u)
+        t = r * high + u
+        l2_send[t] = o.astype(BF16)
+        s2_send[t] = stats(m, l)
         l2_copies.append((
-            u,
-            put(s2_send.at[u], s2_recv.at[u], s2_ss.at[u], s2_rs.at[u], to),
-            put(l2_send.at[u], l2_recv.at[u], l2_ss.at[u], l2_rs.at[u], to),
+            r, t,
+            put(s2_send.at[t], s2_recv.at[t], s2_ss.at[t], s2_rs.at[t], line(u)),
+            put(l2_send.at[t], l2_recv.at[t], l2_ss.at[t], l2_rs.at[t], line(u)),
         ))
 
-    for n, u in enumerate(order):
-        work(u)
-        if n >= 1:
-            forward(order[n - 1])
-
-    o, m, l = gather_plane(0)
-    if scatter:
-        parts = [(o, m, l)]
-        for u, first, second in l2_copies:
-            first.wait_recv()
-            second.wait_recv()
-            parts.append((l2_recv[u].astype(F32), s2_recv[u, 0:1, :], s2_recv[u, 1:2, :]))
-    else:
-        l2_send[0] = o.astype(BF16)
-        s2_send[0] = stats(m, l)
-        l2_recv[hi] = o.astype(BF16)
-        s2_recv[hi] = stats(m, l)
-        for s in range(1, high):
-            put(s2_send.at[0], s2_recv.at[hi], s2_ss.at[s], s2_rs.at[hi], line(s))
-            put(l2_send.at[0], l2_recv.at[hi], l2_ss.at[s], l2_rs.at[hi], line(s))
-        for s in range(1, high):
-            other = lax.rem(hi + s, high)
-            for src, dst, ss, rs in (
-                (s2_send, s2_recv, s2_ss, s2_rs), (l2_send, l2_recv, l2_ss, l2_rs),
-            ):
-                pltpu.make_async_remote_copy(
-                    src_ref=src.at[0], dst_ref=dst.at[other], send_sem=ss.at[s],
-                    recv_sem=rs.at[other], device_id=line(s), device_id_type=MESH,
-                ).wait_recv()
-        parts = [
-            (l2_recv[j].astype(F32), s2_recv[j, 0:1, :], s2_recv[j, 1:2, :]) for j in range(high)
-        ]
-    o, m, l = combine(parts, coef)
-    result = o * (1.0 / l)
-    mine = lo * chunk + sub_of(0) * piece
-    for j in range(piece // LANES):
-        at = pl.ds(pl.multiple_of(mine + j * LANES, LANES), LANES)
-        out_ref[:, at] = result[:, j * LANES:(j + 1) * LANES].T.astype(BF16)
+    def gather_line(r):
+        o, m, l = gather_plane(r, 0)
+        base = r * high
+        if scatter:
+            parts = [(o, m, l)]
+            for n, t, first, second in l2_copies:
+                if n == r:
+                    first.wait_recv()
+                    second.wait_recv()
+                    parts.append((l2_recv[t].astype(F32), s2_recv[t, 0:1, :], s2_recv[t, 1:2, :]))
+        else:
+            l2_send[base] = o.astype(BF16)
+            s2_send[base] = stats(m, l)
+            l2_recv[base + hi] = o.astype(BF16)
+            s2_recv[base + hi] = stats(m, l)
+            for s in range(1, high):
+                put(s2_send.at[base], s2_recv.at[base + hi], s2_ss.at[base + s],
+                    s2_rs.at[base + hi], line(s))
+                put(l2_send.at[base], l2_recv.at[base + hi], l2_ss.at[base + s],
+                    l2_rs.at[base + hi], line(s))
+            for s in range(1, high):
+                other = base + lax.rem(hi + s, high)
+                for src, dst, ss, rs in (
+                    (s2_send, s2_recv, s2_ss, s2_rs), (l2_send, l2_recv, l2_ss, l2_rs),
+                ):
+                    pltpu.make_async_remote_copy(
+                        src_ref=src.at[base], dst_ref=dst.at[other], send_sem=ss.at[base + s],
+                        recv_sem=rs.at[other], device_id=line(s), device_id_type=MESH,
+                    ).wait_recv()
+            parts = [
+                (l2_recv[base + j].astype(F32), s2_recv[base + j, 0:1, :],
+                 s2_recv[base + j, 1:2, :])
+                for j in range(high)
+            ]
+        return combine(parts, coef)
 
     def block(column):
         return out_ref.at[:, pl.ds(pl.multiple_of(column, LANES), piece)]
 
-    if scatter:
-        for s in range(1, high):
-            put(block(mine), block(mine), g2_ss.at[s], g2_rs.at[s], line(s))
-
-    half = piece // 2
-
-    def part(column, h):
-        return out_ref.at[:, pl.ds(pl.multiple_of(column + h * half, LANES), half)]
-
-    across = {p: (hi * PLANE + flip(lo, p), kv) for p in (1, 2)}
-
-    def from_line(s):
-        return lo * chunk + lax.rem(hi - s + high, high) * piece if scatter else lo * chunk
-
-    def beside(s, p):
-        return from_line(s) + (flip(lo, p) - lo) * chunk
+    def from_line(r, s, p=0):
+        part = flip(lo, p) if p else lo
+        return place(part, lax.rem(hi - s + high, high) if scatter else 0, r)
 
     def await_copy(view, ss, rs):
         pltpu.make_async_remote_copy(
@@ -387,39 +385,66 @@
             device_id=line(1), device_id_type=MESH,
         ).wait_recv()
 
-    def to_plane(s):
-        view = block(from_line(s))
+    def to_plane(r, s):
+        view, t = block(from_line(r, s)), r * subs + s
         for p in (1, 2):
-            put(view, view, g1_ss.at[p, s], g1_rs.at[p, s], across[p])
-
-    def pass_on(s):
-        for p, h, over, slot in ((1, 0, 2, 3), (2, 1, 1, 0)):
-            await_copy(block(beside(s, p)), g1_ss.at[p, s], g1_rs.at[p, s])
-            view = part(beside(s, p), h)
-            put(view, view, g1_ss.at[slot, s], g1_rs.at[slot, s], across[over])
-
-    to_plane(0)
+            put(view, view, g1_ss.at[p, t], g1_rs.at[p, t], across[p])
+
+    def finish(r):
+        o, _, l = gather_line(r)
+        result = o * (1.0 / l)
+        mine = from_line(r, 0)
+        for j in range(piece // LANES):
+            at = pl.ds(pl.multiple_of(mine + j * LANES, LANES), LANES)
+            out_ref[:, at] = result[:, j * LANES:(j + 1) * LANES].T.astype(BF16)
+        if scatter:
+            for s in range(1, high):
+                t = r * high + s
+                put(block(mine), block(mine), g2_ss.at[t], g2_rs.at[t], line(s))
+        to_plane(r, 0)
+
+    def spread_line(r, s):
+        t = r * high + s
+        await_copy(block(from_line(r, s)), g2_ss.at[t], g2_rs.at[t])
+        to_plane(r, s)
+
+    def pass_on(r, s):
+        p = 1 + (r + s) % 2
+        t = r * subs + s
+        view = block(from_line(r, s, p))
+        await_copy(view, g1_ss.at[p, t], g1_rs.at[p, t])
+        put(view, view, g1_ss.at[3, t], g1_rs.at[3, t], across[3 - p])
+
+    def last_waits(r, s):
+        t = r * subs + s
+        for p in (2 - (r + s) % 2, 3):
+            await_copy(block(from_line(r, s, p)), g1_ss.at[p, t], g1_rs.at[p, t])
+
+    order = list(range(1, subs)) + [0]
+    pending = []
+    for r in range(rounds):
+        for n, u in enumerate(order):
+            work(r, u)
+            if n >= 1:
+                forward(r, order[n - 1])
+            for step in pending[n::subs]:
+                step()
+        if r < rounds - 1:
+            pending = [functools.partial(finish, r)]
+            pending += [functools.partial(spread_line, r, s) for s in range(1, subs)]
+    finish(rounds - 1)
+    for s in range(subs):
+        for r in range(rounds - 1):
+            pass_on(r, s)
     for s in range(1, subs):
-        await_copy(block(from_line(s)), g2_ss.at[s], g2_rs.at[s])
-        to_plane(s)
-        pass_on(s - 1)
-    pass_on(subs - 1)
-    for s in range(subs):
-        for h, slot in ((0, 3), (1, 0)):
-            await_copy(part(beside(s, 3), h), g1_ss.at[slot, s], g1_rs.at[slot, s])
+        spread_line(rounds - 1, s)
+        pass_on(rounds - 1, s - 1)
+    pass_on(rounds - 1, subs - 1)
+    for r in range(rounds):
+        for s in range(subs):
+            last_waits(r, s)
     for copy in sent:
         copy.wait_send()
-
-
-def write_out(mk_ref, mv_ref, out_ref, mk_hbm, mv_hbm, out_hbm, sems):
-    copies = [
-        pltpu.make_async_copy(src, dst, sems.at[n])
-        for n, (src, dst) in enumerate(((out_ref, out_hbm), (mk_ref, mk_hbm), (mv_ref, mv_hbm)))
-    ]
-    for copy in copies:
-        copy.start()
-    for copy in copies:
-        copy.wait()
 
 
 def per_device(cache_keys, cache_values, importance, assignment, queries):
@@ -429,14 +454,16 @@
     lanes = queries.shape[1]
     high = shards // PLANE
     subs = high if (lanes // PLANE) % (high * LANES) == 0 else 1
-    piece = lanes // PLANE // subs
+    rounds = 2 if (lanes // PLANE // subs) % (2 * LANES) == 0 else 1
+    piece = lanes // PLANE // subs // rounds
+    steps = rounds * subs
     heads = width // LANES
     slots = 2 * NEAR + shards
     wide = 2 * width + 3 * LANES
     dma = pltpu.SemaphoreType.DMA
     vmem = pl.BlockSpec(memory_space=pltpu.VMEM)
     hbm = pl.BlockSpec(memory_space=pltpu.HBM)
-    body = functools.partial(kernel, shards, kv_size, subs, piece)
+    body = functools.partial(kernel, shards, kv_size, subs, rounds, piece)
     shapes = (
         jax.ShapeDtypeStruct((rows, width), BF16),
         jax.ShapeDtypeStruct((rows, width), BF16),
@@ -466,39 +493,32 @@
             pltpu.VMEM((2 * LANES, lanes), BF16),
             pltpu.VMEM((heads, rows, 2 * LANES), BF16),
             pltpu.VMEM((heads, LANES + 16, rows), BF16),
-            pltpu.VMEM((PLANE, subs, LANES, piece), BF16),
-            pltpu.VMEM((PLANE, subs, LANES, piece), BF16),
-            pltpu.VMEM((PLANE, subs, 8, piece), F32),
-            pltpu.VMEM((PLANE, subs, 8, piece), F32),
-            pltpu.VMEM((subs, LANES, piece), F32),
-            pltpu.VMEM((subs, 8, piece), F32),
-            pltpu.VMEM((high, LANES, piece), BF16),
-            pltpu.VMEM((high, LANES, piece), BF16),
-            pltpu.VMEM((high, 8, piece), F32),
-            pltpu.VMEM((high, 8, piece), F32),
+            pltpu.VMEM((PLANE, steps, LANES, piece), BF16),
+            pltpu.VMEM((PLANE, steps, LANES, piece), BF16),
+            pltpu.VMEM((PLANE, steps, 8, piece), F32),
+            pltpu.VMEM((PLANE, steps, 8, piece), F32),
+            pltpu.VMEM((steps, LANES, piece), F32),
+            pltpu.VMEM((steps, 8, piece), F32),
+            pltpu.VMEM((rounds * high, LANES, piece), BF16),
+            pltpu.VMEM((rounds * high, LANES, piece), BF16),
+            pltpu.VMEM((rounds * high, 8, piece), F32),
+            pltpu.VMEM((rounds * high, 8, piece), F32),
             dma((kv_size,)), dma((kv_size,)),
             dma((2,)), dma((2,)),
             dma((shards,)), dma((shards,)),
-            dma((PLANE, subs)), dma((PLANE, subs)),
-            dma((PLANE, subs)), dma((PLANE, subs)),
-            dma((high,)), dma((high,)),
-            dma((high,)), dma((high,)),
-            dma((high,)), dma((high,)),
-            dma((PLANE, subs)), dma((PLANE, subs)),
+            dma((PLANE, steps)), dma((PLANE, steps)),
+            dma((PLANE, steps)), dma((PLANE, steps)),
+            dma((rounds * high,)), dma((rounds * high,)),
+            dma((rounds * high,)), dma((rounds * high,)),
+            dma((rounds * high,)), dma((rounds * high,)),
+            dma((PLANE, steps)), dma((PLANE, steps)),
         ],
         compiler_params=pltpu.CompilerParams(
             collective_id=0, has_side_effects=True, vmem_limit_bytes=40 * 1024 * 1024
         ),
     )
     operands = (cache_keys, cache_values, importance, assignment.reshape(1, rows), queries)
-    results = call(*(pltpu.with_memory_space_constraint(x, pltpu.HBM) for x in operands))
-    return pl.pallas_call(
-        write_out,
-        out_shape=shapes,
-        in_specs=[vmem] * 3,
-        out_specs=(hbm,) * 3,
-        scratch_shapes=[dma((3,))],
-    )(*results)
+    return call(*(pltpu.with_memory_space_constraint(x, pltpu.HBM) for x in operands))
 
 
 def solution(mesh):

time: 54.1 us -> 58.5 us (1.081)
  Pallas kernels: 50.7 us -> 55.1 us
    pallas_call x1, Pallas kernels: 47.8 us -> 55.1 us  [per_device(): call(*(pltpu.with_memory_space_constraint(x, pltpu.HBM) for x in operands))]
    pallas_call x1 -> x0, Pallas kernels: 2.88 us -> none  [per_device(): pl.pallas_call(write_out, out_shape=shapes, in_specs=[vmem] * 3, out_spec...]
    unnamed x6 -> x3, local copies, waits for them, and re-layouts: 2.55 us -> 2.56 us
where the time goes in v4:
time: 58.5 us; the launch traced here: 58.3 us
  Pallas kernels  55.1 us (94%)
  local copies, waits for them, and re-layouts  2.56 us (4%)
  between operations  0.64 us (1%)
    pallas_call x1, Pallas kernels, per_device(): call(*(pltpu.with_memory_space_constraint(x, pltpu.HBM) for x in operands))  55.1 us
    unnamed x3, local copies, waits for them, and re-layouts  2.56 us

profile of v4, /device:TPU:0, one launch (start us, length us, event | category | flops | bytes accessed | tf_op | source)
XLA Modules:
  0.0 58.3 jit_solution(1656760632246073411)
XLA Ops:
  0.6 55.1 %shard_map.76 = (bf16[512,512]{1,0:T(8,128)(2,1)S(1)}, bf16[512,512]{1,0:T(8,128)(2,1)S(1)}, bf16[128,4096]{1,0:T(8,128)(2,1)S(1)}) custom-call(bf16[512,512]{1,0:T(8,128)(2,1)} %k_hbm.1, bf16[512,512]{1,0:T(8,128)(2,1)} %v_hbm.1, bf16[4,512]{1,0:T(4,128)(2,1)} %imp_hbm.1, s32[1,512]{1,0:T(1,128)} %bitcast.1, bf16[128,4096]{1,0:T(8,128)(2,1)} %q_hbm.1), custom_call_target="tpu_custom_call" | custom-call | tf_op jit(solution)/shard_map/pallas_call | solution.py:521
  55.8 0.8 %copy.11 = bf16[512,512]{1,0:T(8,128)(2,1)} copy(bf16[512,512]{1,0:T(8,128)(2,1)S(1)} %get-tuple-element.3) | data formatting | bytes 1048576
  56.6 0.8 %copy.12 = bf16[512,512]{1,0:T(8,128)(2,1)} copy(bf16[512,512]{1,0:T(8,128)(2,1)S(1)} %get-tuple-element.4) | data formatting | bytes 1048576
  57.4 1.0 %copy.13 = bf16[128,4096]{1,0:T(8,128)(2,1)} copy(bf16[128,4096]{1,0:T(8,128)(2,1)S(1)} %get-tuple-element.5) | data formatting | bytes 2097152

commit v5 on v4

--- a/solution.py
+++ b/solution.py
@@ -273,14 +273,21 @@
         v_t[h, 0:LANES, :] = value.T
         v_t[h, LANES:, :] = jnp.ones((16, rows), BF16)
 
-    def attend(column):
-        h = lax.div(column, group_lanes)
-        queries = q_t[:, pl.ds(pl.multiple_of(column, LANES), piece)]
-        score = dot(k_ext[h], queries)
-        peak = jnp.max(score, axis=0, keepdims=True)
-        prob = jnp.exp2((score - peak) * coef).astype(BF16)
-        both = dot(v_t[h], prob)
-        return both[0:LANES], peak, both[LANES:LANES + 1]
+    def attend(columns):
+        def score_of(column):
+            queries = q_t[:, pl.ds(pl.multiple_of(column, LANES), piece)]
+            return dot(k_ext[lax.div(column, group_lanes)], queries)
+
+        results = []
+        score = score_of(columns[0])
+        for n, column in enumerate(columns):
+            ahead = score_of(columns[n + 1]) if n + 1 < len(columns) else None
+            peak = jnp.max(score, axis=0, keepdims=True)
+            prob = jnp.exp2((score - peak) * coef).astype(BF16)
+            both = dot(v_t[lax.div(column, group_lanes)], prob)
+            results.append((both[0:LANES], peak, both[LANES:LANES + 1]))
+            score = ahead
+        return results
 
     def sub_of(u):
         return lax.rem(hi + u, high) if scatter else 0
@@ -294,58 +301,78 @@
         return (lax.rem(hi + s, high) * PLANE + lo, kv)
 
     across = {p: (hi * PLANE + flip(lo, p), kv) for p in (1, 2, 3)}
-    l1_copies = {}
-
-    def work(r, u):
-        t = r * subs + u
-        for s in (3, 1, 2, 0):
-            dest = flip(lo, s) if s else lo
-            o, m, l = attend(place(dest, sub_of(u), r))
+
+    def hop(s, t):
+        return [
+            pltpu.make_async_remote_copy(
+                src_ref=src.at[s, t], dst_ref=dst.at[s, t], send_sem=ss.at[s, t],
+                recv_sem=rs.at[s, t], device_id=across[s], device_id_type=MESH,
+            )
+            for src, dst, ss, rs in (
+                (s1_send, s1_recv, s1_ss, s1_rs), (l1_send, l1_recv, l1_ss, l1_rs),
+            )
+        ]
+
+    def hop_line(t):
+        return [
+            pltpu.make_async_remote_copy(
+                src_ref=src.at[t], dst_ref=dst.at[t], send_sem=ss.at[t],
+                recv_sem=rs.at[t], device_id=line(t), device_id_type=MESH,
+            )
+            for src, dst, ss, rs in (
+                (s2_send, s2_recv, s2_ss, s2_rs), (l2_send, l2_recv, l2_ss, l2_rs),
+            )
+        ]
+
+    def work(t):
+        steps = (3, 1, 2, 0)
+        places = [place(flip(lo, s) if s else lo, sub_of(t), 0) for s in steps]
+        for s, (o, m, l) in zip(steps, attend(places)):
             if s == 0:
                 own_o[t] = o
                 own_s[t] = stats(m, l)
-                continue
-            l1_send[s, t] = o.astype(BF16)
-            s1_send[s, t] = stats(m, l)
-            l1_copies[s, t] = (
-                put(s1_send.at[s, t], s1_recv.at[s, t], s1_ss.at[s, t], s1_rs.at[s, t], across[s]),
-                put(l1_send.at[s, t], l1_recv.at[s, t], l1_ss.at[s, t], l1_rs.at[s, t], across[s]),
-            )
-
-    def gather_plane(r, u):
-        t = r * subs + u
+            else:
+                l1_send[s, t] = o.astype(BF16)
+                s1_send[s, t] = stats(m, l)
+        for s in (3, 1, 2):
+            for copy in hop(s, t):
+                copy.start()
+
+    def gather_plane(t):
         parts = [(own_o[t], own_s[t, 0:1, :], own_s[t, 1:2, :])]
         for s in (1, 2, 3):
-            for copy in l1_copies[s, t]:
+            for copy in hop(s, t):
                 copy.wait_recv()
             parts.append(
                 (l1_recv[s, t].astype(F32), s1_recv[s, t, 0:1, :], s1_recv[s, t, 1:2, :])
             )
         return combine(parts, coef)
 
-    l2_copies = []
-
-    def forward(r, u):
-        o, m, l = gather_plane(r, u)
-        t = r * high + u
+    def forward(t):
+        o, m, l = gather_plane(t)
         l2_send[t] = o.astype(BF16)
         s2_send[t] = stats(m, l)
-        l2_copies.append((
-            r, t,
-            put(s2_send.at[t], s2_recv.at[t], s2_ss.at[t], s2_rs.at[t], line(u)),
-            put(l2_send.at[t], l2_recv.at[t], l2_ss.at[t], l2_rs.at[t], line(u)),
-        ))
+        for copy in hop_line(t):
+            copy.start()
+
+    def turn(n, carry):
+        work(lax.rem(n + 1, subs))
+
+        @pl.when(n >= 1)
+        def _():
+            forward(n)
+
+        return carry
 
     def gather_line(r):
-        o, m, l = gather_plane(r, 0)
+        o, m, l = gather_plane(0)
         base = r * high
         if scatter:
             parts = [(o, m, l)]
-            for n, t, first, second in l2_copies:
-                if n == r:
-                    first.wait_recv()
-                    second.wait_recv()
-                    parts.append((l2_recv[t].astype(F32), s2_recv[t, 0:1, :], s2_recv[t, 1:2, :]))
+            for t in range(1, high):
+                for copy in hop_line(t):
+                    copy.wait_recv()
+                parts.append((l2_recv[t].astype(F32), s2_recv[t, 0:1, :], s2_recv[t, 1:2, :]))
         else:
             l2_send[base] = o.astype(BF16)
             s2_send[base] = stats(m, l)
@@ -420,18 +447,7 @@
         for p in (2 - (r + s) % 2, 3):
             await_copy(block(from_line(r, s, p)), g1_ss.at[p, t], g1_rs.at[p, t])
 
-    order = list(range(1, subs)) + [0]
-    pending = []
-    for r in range(rounds):
-        for n, u in enumerate(order):
-            work(r, u)
-            if n >= 1:
-                forward(r, order[n - 1])
-            for step in pending[n::subs]:
-                step()
-        if r < rounds - 1:
-            pending = [functools.partial(finish, r)]
-            pending += [functools.partial(spread_line, r, s) for s in range(1, subs)]
+    lax.fori_loop(0, subs, turn, 0)
     finish(rounds - 1)
     for s in range(subs):
         for r in range(rounds - 1):
@@ -446,6 +462,19 @@
     for copy in sent:
         copy.wait_send()
 
+    def drain(t, carry):
+        for s in (1, 2, 3):
+            for copy in hop(s, t):
+                copy.wait_send()
+        if scatter:
+            @pl.when(t >= 1)
+            def _():
+                for copy in hop_line(t):
+                    copy.wait_send()
+        return carry
+
+    lax.fori_loop(0, subs, drain, 0)
+
 
 def per_device(cache_keys, cache_values, importance, assignment, queries):
     shards = lax.axis_size("ctx")
@@ -454,7 +483,7 @@
     lanes = queries.shape[1]
     high = shards // PLANE
     subs = high if (lanes // PLANE) % (high * LANES) == 0 else 1
-    rounds = 2 if (lanes // PLANE // subs) % (2 * LANES) == 0 else 1
+    rounds = 1
     piece = lanes // PLANE // subs // rounds
     steps = rounds * subs
     heads = width // LANES

time: 58.5 us -> 50.2 us (0.86)
  Pallas kernels: 55.1 us -> 46.8 us
    pallas_call x1, Pallas kernels: 55.1 us -> 46.8 us  [per_device(): call(*(pltpu.with_memory_space_constraint(x, pltpu.HBM) for x in operands))]
where the time goes in v5:
time: 50.2 us; the launch traced here: 50 us
  Pallas kernels  46.8 us (93%)
  local copies, waits for them, and re-layouts  2.56 us (5%)
  between operations  0.64 us (1%)
    pallas_call x1, Pallas kernels, per_device(): call(*(pltpu.with_memory_space_constraint(x, pltpu.HBM) for x in operands))  46.8 us
    unnamed x3, local copies, waits for them, and re-layouts  2.56 us

profile of v5, /device:TPU:0, one launch (start us, length us, event | category | flops | bytes accessed | tf_op | source)
XLA Modules:
  0.0 50.0 jit_solution(16343684860437335086)
XLA Ops:
  0.6 46.8 %shard_map.76 = (bf16[512,512]{1,0:T(8,128)(2,1)S(1)}, bf16[512,512]{1,0:T(8,128)(2,1)S(1)}, bf16[128,4096]{1,0:T(8,128)(2,1)S(1)}) custom-call(bf16[512,512]{1,0:T(8,128)(2,1)} %k_hbm.1, bf16[512,512]{1,0:T(8,128)(2,1)} %v_hbm.1, bf16[4,512]{1,0:T(4,128)(2,1)} %imp_hbm.1, s32[1,512]{1,0:T(1,128)} %bitcast.1, bf16[128,4096]{1,0:T(8,128)(2,1)} %q_hbm.1), custom_call_target="tpu_custom_call" | custom-call | tf_op jit(solution)/shard_map/pallas_call | solution.py:550
  47.5 0.8 %copy.11 = bf16[512,512]{1,0:T(8,128)(2,1)} copy(bf16[512,512]{1,0:T(8,128)(2,1)S(1)} %get-tuple-element.3) | data formatting | bytes 1048576
  48.3 0.8 %copy.12 = bf16[512,512]{1,0:T(8,128)(2,1)} copy(bf16[512,512]{1,0:T(8,128)(2,1)S(1)} %get-tuple-element.4) | data formatting | bytes 1048576
  49.0 1.0 %copy.13 = bf16[128,4096]{1,0:T(8,128)(2,1)} copy(bf16[128,4096]{1,0:T(8,128)(2,1)S(1)} %get-tuple-element.5) | data formatting | bytes 2097152

commit v6 on v5

--- a/solution.py
+++ b/solution.py
@@ -116,6 +116,12 @@
         far_recv[s] = jnp.zeros((16, LANES), BF16)
     far_wide[...] = jnp.zeros_like(far_wide)
 
+    pl.semaphore_wait(barrier, shards - 1 + kv_size - 1)
+    kv_copies = [
+        put(kv_send, kv_recv.at[s], kv_ss.at[s], kv_rs.at[s], (me, lax.rem(kv + s, kv_size)))
+        for s in range(1, kv_size)
+    ]
+
     asg_in.wait()
     asg = asg_ref[...]
     owner = jnp.right_shift(asg, rows.bit_length() - 1)
@@ -142,12 +148,6 @@
     chosen = jnp.concatenate(
         [select(key_next, NEAR), select(key_prev, NEAR), select(far, shards)], axis=0
     )
-    pl.semaphore_wait(barrier, shards - 1 + kv_size - 1)
-    kv_copies = [
-        put(kv_send, kv_recv.at[s], kv_ss.at[s], kv_rs.at[s], (me, lax.rem(kv + s, kv_size)))
-        for s in range(1, kv_size)
-    ]
-
     chosen_b = chosen.astype(BF16)
     k_in.wait()
     v_in.wait()
@@ -358,9 +358,9 @@
     def turn(n, carry):
         work(lax.rem(n + 1, subs))
 
-        @pl.when(n >= 1)
+        @pl.when(n >= 2)
         def _():
-            forward(n)
+            forward(n - 1)
 
         return carry
 
@@ -412,9 +412,12 @@
             device_id=line(1), device_id_type=MESH,
         ).wait_recv()
 
+    def straight(s):
+        return s >= 2
+
     def to_plane(r, s):
         view, t = block(from_line(r, s)), r * subs + s
-        for p in (1, 2):
+        for p in (3, 1, 2) if straight(s) else (1, 2):
             put(view, view, g1_ss.at[p, t], g1_rs.at[p, t], across[p])
 
     def finish(r):
@@ -436,6 +439,8 @@
         to_plane(r, s)
 
     def pass_on(r, s):
+        if straight(s):
+            return
         p = 1 + (r + s) % 2
         t = r * subs + s
         view = block(from_line(r, s, p))
@@ -444,10 +449,12 @@
 
     def last_waits(r, s):
         t = r * subs + s
-        for p in (2 - (r + s) % 2, 3):
+        for p in (1, 2, 3) if straight(s) else (2 - (r + s) % 2, 3):
             await_copy(block(from_line(r, s, p)), g1_ss.at[p, t], g1_rs.at[p, t])
 
     lax.fori_loop(0, subs, turn, 0)
+    if scatter:
+        forward(subs - 1)
     finish(rounds - 1)
     for s in range(subs):
         for r in range(rounds - 1):

time: 50.2 us -> 49.7 us (0.990)
  no operation moved by 1% of the time
where the time goes in v6:
time: 49.7 us; the launch traced here: 49.5 us
  Pallas kernels  46.3 us (93%)
  local copies, waits for them, and re-layouts  2.56 us (5%)
  between operations  0.64 us (1%)
    pallas_call x1, Pallas kernels, per_device(): call(*(pltpu.with_memory_space_constraint(x, pltpu.HBM) for x in operands))  46.3 us
    unnamed x3, local copies, waits for them, and re-layouts  2.56 us

profile of v6, /device:TPU:0, one launch (start us, length us, event | category | flops | bytes accessed | tf_op | source)
XLA Modules:
  0.0 49.5 jit_solution(6333961025291578514)
XLA Ops:
  0.6 46.3 %shard_map.76 = (bf16[512,512]{1,0:T(8,128)(2,1)S(1)}, bf16[512,512]{1,0:T(8,128)(2,1)S(1)}, bf16[128,4096]{1,0:T(8,128)(2,1)S(1)}) custom-call(bf16[512,512]{1,0:T(8,128)(2,1)} %k_hbm.1, bf16[512,512]{1,0:T(8,128)(2,1)} %v_hbm.1, bf16[4,512]{1,0:T(4,128)(2,1)} %imp_hbm.1, s32[1,512]{1,0:T(1,128)} %bitcast.1, bf16[128,4096]{1,0:T(8,128)(2,1)} %q_hbm.1), custom_call_target="tpu_custom_call" | custom-call | tf_op jit(solution)/shard_map/pallas_call | solution.py:557
  47.0 0.8 %copy.11 = bf16[512,512]{1,0:T(8,128)(2,1)} copy(bf16[512,512]{1,0:T(8,128)(2,1)S(1)} %get-tuple-element.3) | data formatting | bytes 1048576
  47.8 0.8 %copy.12 = bf16[512,512]{1,0:T(8,128)(2,1)} copy(bf16[512,512]{1,0:T(8,128)(2,1)S(1)} %get-tuple-element.4) | data formatting | bytes 1048576
  48.6 1.0 %copy.13 = bf16[128,4096]{1,0:T(8,128)(2,1)} copy(bf16[128,4096]{1,0:T(8,128)(2,1)S(1)} %get-tuple-element.5) | data formatting | bytes 2097152

commit v7 on v6

--- a/solution.py
+++ b/solution.py
@@ -278,16 +278,14 @@
             queries = q_t[:, pl.ds(pl.multiple_of(column, LANES), piece)]
             return dot(k_ext[lax.div(column, group_lanes)], queries)
 
-        results = []
         score = score_of(columns[0])
         for n, column in enumerate(columns):
             ahead = score_of(columns[n + 1]) if n + 1 < len(columns) else None
             peak = jnp.max(score, axis=0, keepdims=True)
             prob = jnp.exp2((score - peak) * coef).astype(BF16)
             both = dot(v_t[lax.div(column, group_lanes)], prob)
-            results.append((both[0:LANES], peak, both[LANES:LANES + 1]))
+            yield both[0:LANES], peak, both[LANES:LANES + 1]
             score = ahead
-        return results
 
     def sub_of(u):
         return lax.rem(hi + u, high) if scatter else 0
@@ -334,9 +332,8 @@
             else:
                 l1_send[s, t] = o.astype(BF16)
                 s1_send[s, t] = stats(m, l)
-        for s in (3, 1, 2):
-            for copy in hop(s, t):
-                copy.start()
+                for copy in hop(s, t):
+                    copy.start()
 
     def gather_plane(t):
         parts = [(own_o[t], own_s[t, 0:1, :], own_s[t, 1:2, :])]

time: 49.7 us -> 49.1 us (0.988)
  Pallas kernels: 46.3 us -> 45.7 us
    pallas_call x1, Pallas kernels: 46.3 us -> 45.7 us  [per_device(): call(*(pltpu.with_memory_space_constraint(x, pltpu.HBM) for x in operands))]
where the time goes in v7:
time: 49.1 us; the launch traced here: 48.9 us
  Pallas kernels  45.7 us (93%)
  local copies, waits for them, and re-layouts  2.56 us (5%)
  between operations  0.64 us (1%)
    pallas_call x1, Pallas kernels, per_device(): call(*(pltpu.with_memory_space_constraint(x, pltpu.HBM) for x in operands))  45.7 us
    unnamed x3, local copies, waits for them, and re-layouts  2.56 us

profile of v7, /device:TPU:0, one launch (start us, length us, event | category | flops | bytes accessed | tf_op | source)
XLA Modules:
  0.0 48.9 jit_solution(13591049158101980106)
XLA Ops:
  0.6 45.7 %shard_map.76 = (bf16[512,512]{1,0:T(8,128)(2,1)S(1)}, bf16[512,512]{1,0:T(8,128)(2,1)S(1)}, bf16[128,4096]{1,0:T(8,128)(2,1)S(1)}) custom-call(bf16[512,512]{1,0:T(8,128)(2,1)} %k_hbm.1, bf16[512,512]{1,0:T(8,128)(2,1)} %v_hbm.1, bf16[4,512]{1,0:T(4,128)(2,1)} %imp_hbm.1, s32[1,512]{1,0:T(1,128)} %bitcast.1, bf16[128,4096]{1,0:T(8,128)(2,1)} %q_hbm.1), custom_call_target="tpu_custom_call" | custom-call | tf_op jit(solution)/shard_map/pallas_call | solution.py:554
  46.3 0.8 %copy.11 = bf16[512,512]{1,0:T(8,128)(2,1)} copy(bf16[512,512]{1,0:T(8,128)(2,1)S(1)} %get-tuple-element.3) | data formatting | bytes 1048576
  47.1 0.8 %copy.12 = bf16[512,512]{1,0:T(8,128)(2,1)} copy(bf16[512,512]{1,0:T(8,128)(2,1)S(1)} %get-tuple-element.4) | data formatting | bytes 1048576
  47.9 1.0 %copy.13 = bf16[128,4096]{1,0:T(8,128)(2,1)} copy(bf16[128,4096]{1,0:T(8,128)(2,1)S(1)} %get-tuple-element.5) | data formatting | bytes 2097152
